TPU v7x, 1024 devices: a whole 4x8x16 slice. The times are simulated.
1024 devices in a mesh: wide: 16 (over y, core), narrow: 64 (over z, x).
Axes of the slice: x: 4, y: 8, z: 16, core: 2. Of those that a mesh axis runs over, the one named last changes fastest.
Arguments:
- forcing: float32 [512, 2048, 128], P('wide', 'narrow'), may hold values from -8 to 8
- classes: int32 [512, 2048], P('wide', 'narrow'), may hold values from 0 to 3
- drag: float32 [4], replicated, may hold values from 0.02 to 50
- depth: float32 [128], replicated, may hold values from 0.5 to 2
Outputs:
- pressure: float32 [512, 2048, 128], P('wide', 'narrow')
All inputs are finite; a program needn't handle non-finite values.
Results may differ from a plain program's by a relative error of at most 0.0001.
Values sent between devices are 32-bit elements; how exact they have to be, the bound alone decides.
A program may use at most 32 MiB of HBM per device.

v0:
```python
import jax
import jax.numpy as jnp
from jax import lax
from jax.sharding import PartitionSpec as P

relax = 0.8


def with_halo(block, sides, width):
    for axis, dim in sides:
        count = lax.axis_size(axis)
        forward = [(i, i + 1) for i in range(count - 1)]
        backward = [(target, source) for source, target in forward]
        low = lax.ppermute(
            lax.slice_in_dim(block, block.shape[dim] - width, None, axis=dim), axis, forward
        )
        high = lax.ppermute(lax.slice_in_dim(block, 0, width, axis=dim), axis, backward)
        block = jnp.concatenate([low, block, high], axis=dim)
    return block


def vertical_terms(depth):
    coupling = 2.0 / (depth[:-1] + depth[1:])
    zero = jnp.zeros((1,), depth.dtype)
    return (jnp.concatenate([coupling, zero]), jnp.concatenate([zero, coupling]))


def apply_padded(padded, drag_cells, depth, upper, lower):
    centre = padded[1:-1, 1:-1]
    horiz = (
        4.0 * centre - padded[2:, 1:-1] - padded[:-2, 1:-1] - padded[1:-1, 2:] - padded[1:-1, :-2]
    )
    zero = jnp.zeros(centre.shape[:2] + (1,), centre.dtype)
    above = jnp.concatenate([centre[:, :, 1:], zero], axis=2)
    below = jnp.concatenate([zero, centre[:, :, :-1]], axis=2)
    return (
        depth * (horiz + drag_cells[:, :, None] * centre)
        + upper * (centre - above)
        + lower * (centre - below)
    )


def coarse_solve(rhs, tile_drag, cx, cy):
    blocks = rhs.shape[1]
    rows = jnp.arange(blocks)[:, None]
    cols = jnp.arange(blocks)[None, :]
    eye = jnp.where(rows == cols, 1.0, 0.0).astype(jnp.float32)
    beside = jnp.where(jnp.abs(rows - cols) == 1, 1.0, 0.0).astype(jnp.float32)
    base = (2.0 * cx + 2.0 * cy) * eye - cx * beside

    def forward(carry, item):
        inv_prev, g_prev = carry
        rhs_row, drag_row = item
        block = base + eye * drag_row[None, :] - cy * cy * inv_prev
        g_now = rhs_row + cy * jnp.dot(inv_prev, g_prev, precision=lax.Precision.HIGHEST)
        factor = jnp.linalg.cholesky(block)
        half = lax.linalg.triangular_solve(factor, eye, left_side=True, lower=True)
        inverse = lax.linalg.triangular_solve(
            factor, half, left_side=True, lower=True, transpose_a=True
        )
        return ((inverse, g_now), (inverse, g_now))

    start = (jnp.zeros((blocks, blocks), jnp.float32), jnp.zeros((blocks,), jnp.float32))
    _, (inverses, g_all) = lax.scan(forward, start, (rhs, tile_drag))

    def backward(e_next, item):
        inverse, g_now = item
        e_now = jnp.dot(inverse, g_now + cy * e_next, precision=lax.Precision.HIGHEST)
        return (e_now, e_now)

    _, solved = lax.scan(
        backward, jnp.zeros((blocks,), jnp.float32), (inverses, g_all), reverse=True
    )
    return solved


def local(forcing, classes, drag, depth):
    cx, cy, nz = forcing.shape
    kinds = jnp.arange(drag.shape[0])
    drag_cells = jnp.sum(
        jnp.where(classes[:, :, None] == kinds[None, None, :], drag[None, None, :], 0.0), axis=2
    )
    upper, lower = vertical_terms(depth)
    diag = depth * (4.0 + drag_cells[:, :, None]) + upper + lower
    ztotal = jnp.sum(depth)
    drag_sum = (jnp.sum(drag_cells) / (cx * cy)).reshape(1)

    def operate(field):
        padded = with_halo(field, (("wide", 0), ("narrow", 1)), 1)
        return apply_padded(padded, drag_cells, depth, upper, lower)

    first = relax * forcing / diag
    second = first + relax * (forcing - operate(first)) / diag
    residual = forcing - operate(second)
    local_sum = jnp.sum(residual).reshape(1)
    all_res, all_drag = (
        lax.all_gather(local_sum, ("wide", "narrow"), axis=0, tiled=True),
        lax.all_gather(drag_sum, ("wide", "narrow"), axis=0, tiled=True),
    )
    n_wide = lax.axis_size("wide")
    n_narrow = lax.axis_size("narrow")
    correction = coarse_solve(
        all_res.reshape(n_wide, n_narrow) / ztotal, all_drag.reshape(n_wide, n_narrow), cx, cy
    )
    own_value = correction[lax.axis_index("wide"), lax.axis_index("narrow")]
    corrected = second + own_value
    third = corrected + relax * (forcing - operate(corrected)) / diag
    result = third + relax * (forcing - operate(third)) / diag
    return result


def solution(mesh):
    in_specs = (P("wide", "narrow", None), P("wide", "narrow"), P(), P())
    out_specs = P("wide", "narrow", None)
    return jax.shard_map(local, mesh=mesh, in_specs=in_specs, out_specs=out_specs, check_vma=False)
```

profile of v0, /device:TPU:96, one launch (start us, length us, event | category | flops | bytes accessed | tf_op | source)
XLA Modules:
  0.0 430.6 jit_solution(1560415053597625618)
XLA Ops:
  18.0 5.4 %collective-permute-done.3 = f32[34,1,128]{2,1,0:T(1,128)S(1)} collective-permute-done((f32[34,1,128]{2,1,0:T(1,128)S(1)}, f32[34,1,128]{2,1,0:T(1,128)S(1)}, u32[]{:S(2)}, u32[]{:S(2)}) %collective-permute-start.3) | collective-permute-done | bytes 17440 | tf_op jit(solution)/shard_map/ppermute | solution.py:14
  43.7 132.2 %all-reduce.10 = (f32[1024]{0:T(1024)S(1)}, f32[1024]{0:T(1024)S(1)}) all-reduce(f32[1024]{0:T(1024)S(1)} %dynamic-update-slice.3, f32[1024]{0:T(1024)S(1)} %dynamic-update-slice.4), channel_id=1, replica_groups=mesh['wide'=16,'narrow'=64] {'wide','narrow'}, use_global_device_ids=true, to_apply=%add.8 | all-reduce | flops 2048 | bytes 16384
  176.7 209.8 %while.35 = (s32[]{:T(128)}, f32[64,64]{1,0:T(8,128)S(1)}, f32[64]{0:T(128)S(1)}, f32[16,64,64]{2,1,0:T(8,128)S(1)}, f32[16,64]{1,0:T(8,128)S(1)}, /*index=5*/f3...) while((s32[]{:T(128)}, f32[64,64]{1,0:T(8,128)S(1)}, ...), condition=%wide.region_7.8_spmd.clone.clone, body=%wide.region_4.7_spmd.clone.clone.sunk | while | flops 6492418 | bytes 380281 | solution.py:64
  177.0 5.8 %cholesky.78 = f32[64,64]{1,0:T(8,128)S(1)} custom-call(f32[64,64]{1,0:T(8,128)S(1)} %fusion.116), custom_call_target="Cholesky" | custom-call | tf_op jit(solution)/shard_map/while/body/eval_jaxpr/jit(cholesky)/cholesky | solution.py:56
  190.1 5.8 %cholesky.78 = f32[64,64]{1,0:T(8,128)S(1)} custom-call(f32[64,64]{1,0:T(8,128)S(1)} %fusion.116), custom_call_target="Cholesky" | custom-call | tf_op jit(solution)/shard_map/while/body/eval_jaxpr/jit(cholesky)/cholesky | solution.py:56
  197.3 4.9 %custom-call.13 = f32[1,64,64]{1,2,0:T(8,128)S(1)} custom-call(f32[1,64,64]{2,1,0:T(8,128)S(1)} %fusion.117), custom_call_target="InvertDiagBlocksLowerTriangular" | custom-call | tf_op jit(solution)/shard_map/while/body/eval_jaxpr/triangular_solve | solution.py:58
  203.3 5.8 %cholesky.78 = f32[64,64]{1,0:T(8,128)S(1)} custom-call(f32[64,64]{1,0:T(8,128)S(1)} %fusion.116), custom_call_target="Cholesky" | custom-call | tf_op jit(solution)/shard_map/while/body/eval_jaxpr/jit(cholesky)/cholesky | solution.py:56
  216.4 5.8 %cholesky.78 = f32[64,64]{1,0:T(8,128)S(1)} custom-call(f32[64,64]{1,0:T(8,128)S(1)} %fusion.116), custom_call_target="Cholesky" | custom-call | tf_op jit(solution)/shard_map/while/body/eval_jaxpr/jit(cholesky)/cholesky | solution.py:56
  229.5 5.8 %cholesky.78 = f32[64,64]{1,0:T(8,128)S(1)} custom-call(f32[64,64]{1,0:T(8,128)S(1)} %fusion.116), custom_call_target="Cholesky" | custom-call | tf_op jit(solution)/shard_map/while/body/eval_jaxpr/jit(cholesky)/cholesky | solution.py:56
  242.6 5.8 %cholesky.78 = f32[64,64]{1,0:T(8,128)S(1)} custom-call(f32[64,64]{1,0:T(8,128)S(1)} %fusion.116), custom_call_target="Cholesky" | custom-call | tf_op jit(solution)/shard_map/while/body/eval_jaxpr/jit(cholesky)/cholesky | solution.py:56
  249.8 4.9 %custom-call.13 = f32[1,64,64]{1,2,0:T(8,128)S(1)} custom-call(f32[1,64,64]{2,1,0:T(8,128)S(1)} %fusion.117), custom_call_target="InvertDiagBlocksLowerTriangular" | custom-call | tf_op jit(solution)/shard_map/while/body/eval_jaxpr/triangular_solve | solution.py:58
  255.7 5.8 %cholesky.78 = f32[64,64]{1,0:T(8,128)S(1)} custom-call(f32[64,64]{1,0:T(8,128)S(1)} %fusion.116), custom_call_target="Cholesky" | custom-call | tf_op jit(solution)/shard_map/while/body/eval_jaxpr/jit(cholesky)/cholesky | solution.py:56
  268.8 5.8 %cholesky.78 = f32[64,64]{1,0:T(8,128)S(1)} custom-call(f32[64,64]{1,0:T(8,128)S(1)} %fusion.116), custom_call_target="Cholesky" | custom-call | tf_op jit(solution)/shard_map/while/body/eval_jaxpr/jit(cholesky)/cholesky | solution.py:56
  276.0 4.9 %custom-call.13 = f32[1,64,64]{1,2,0:T(8,128)S(1)} custom-call(f32[1,64,64]{2,1,0:T(8,128)S(1)} %fusion.117), custom_call_target="InvertDiagBlocksLowerTriangular" | custom-call | tf_op jit(solution)/shard_map/while/body/eval_jaxpr/triangular_solve | solution.py:58
  281.9 5.8 %cholesky.78 = f32[64,64]{1,0:T(8,128)S(1)} custom-call(f32[64,64]{1,0:T(8,128)S(1)} %fusion.116), custom_call_target="Cholesky" | custom-call | tf_op jit(solution)/shard_map/while/body/eval_jaxpr/jit(cholesky)/cholesky | solution.py:56
  289.1 4.9 %custom-call.13 = f32[1,64,64]{1,2,0:T(8,128)S(1)} custom-call(f32[1,64,64]{2,1,0:T(8,128)S(1)} %fusion.117), custom_call_target="InvertDiagBlocksLowerTriangular" | custom-call | tf_op jit(solution)/shard_map/while/body/eval_jaxpr/triangular_solve | solution.py:58
  295.0 5.8 %cholesky.78 = f32[64,64]{1,0:T(8,128)S(1)} custom-call(f32[64,64]{1,0:T(8,128)S(1)} %fusion.116), custom_call_target="Cholesky" | custom-call | tf_op jit(solution)/shard_map/while/body/eval_jaxpr/jit(cholesky)/cholesky | solution.py:56
  308.1 5.8 %cholesky.78 = f32[64,64]{1,0:T(8,128)S(1)} custom-call(f32[64,64]{1,0:T(8,128)S(1)} %fusion.116), custom_call_target="Cholesky" | custom-call | tf_op jit(solution)/shard_map/while/body/eval_jaxpr/jit(cholesky)/cholesky | solution.py:56
  321.3 5.8 %cholesky.78 = f32[64,64]{1,0:T(8,128)S(1)} custom-call(f32[64,64]{1,0:T(8,128)S(1)} %fusion.116), custom_call_target="Cholesky" | custom-call | tf_op jit(solution)/shard_map/while/body/eval_jaxpr/jit(cholesky)/cholesky | solution.py:56
  334.4 5.8 %cholesky.78 = f32[64,64]{1,0:T(8,128)S(1)} custom-call(f32[64,64]{1,0:T(8,128)S(1)} %fusion.116), custom_call_target="Cholesky" | custom-call | tf_op jit(solution)/shard_map/while/body/eval_jaxpr/jit(cholesky)/cholesky | solution.py:56
  347.5 5.8 %cholesky.78 = f32[64,64]{1,0:T(8,128)S(1)} custom-call(f32[64,64]{1,0:T(8,128)S(1)} %fusion.116), custom_call_target="Cholesky" | custom-call | tf_op jit(solution)/shard_map/while/body/eval_jaxpr/jit(cholesky)/cholesky | solution.py:56
  360.6 5.8 %cholesky.78 = f32[64,64]{1,0:T(8,128)S(1)} custom-call(f32[64,64]{1,0:T(8,128)S(1)} %fusion.116), custom_call_target="Cholesky" | custom-call | tf_op jit(solution)/shard_map/while/body/eval_jaxpr/jit(cholesky)/cholesky | solution.py:56
  373.7 5.8 %cholesky.78 = f32[64,64]{1,0:T(8,128)S(1)} custom-call(f32[64,64]{1,0:T(8,128)S(1)} %fusion.116), custom_call_target="Cholesky" | custom-call | tf_op jit(solution)/shard_map/while/body/eval_jaxpr/jit(cholesky)/cholesky | solution.py:56
  405.7 5.0 %collective-permute-done.11 = f32[34,1,128]{2,1,0:T(1,128)S(1)} collective-permute-done((f32[34,1,128]{2,1,0:T(1,128)S(1)}, f32[34,1,128]{2,1,0:T(1,128)S(1)}, u32[]{:S(2)}, u32[]{:S(2)}) %collective-permute-start.11) | collective-permute-done | bytes 17440 | tf_op jit(solution)/shard_map/ppermute | solution.py:14
  (340 shorter events, 175.6 us)
Async XLA Ops:
  1.4 0.7 copy-start.1
  3.5 4.3 %collective-permute-start = (f32[1,32,128]{2,1,0:T(8,128)S(1)}, f32[1,32,128]{2,1,0:T(8,128)S(1)}, u32[]{:S(2)}, u32[]{:S(2)}) collective-permute-start(f32[1,32,128]{2,1,0:T(8,128)S(1)} %get-tuple-element.265), channel_id=1, source_target_pairs={{64,0},{128,64},{192,128},{256,192},{320,256},{384,320},{448,384},... | collective-permute-start | bytes 49160 | tf_op jit(solution)/shard_map/ppermute | solution.py:17
  5.4 6.3 %collective-permute-start.1 = (f32[1,32,128]{2,1,0:T(8,128)S(1)}, f32[1,32,128]{2,1,0:T(8,128)S(1)}, u32[]{:S(2)}, u32[]{:S(2)}) collective-permute-start(f32[1,32,128]{2,1,0:T(8,128)S(1)} %get-tuple-element.264), channel_id=1, source_target_pairs={{0,64},{64,128},{128,192},{192,256},{256,320},{320,384},{384,448},... | collective-permute-start | bytes 49160 | tf_op jit(solution)/shard_map/ppermute | solution.py:14
  11.7 6.2 %collective-permute-start.2 = (f32[34,1,128]{2,1,0:T(1,128)S(1)}, f32[34,1,128]{2,1,0:T(1,128)S(1)}, u32[]{:S(2)}, u32[]{:S(2)}) collective-permute-start(f32[34,1,128]{2,1,0:T(1,128)S(1)} %get-tuple-element.248), channel_id=1, source_target_pairs={{1,0},{2,1},{3,2},{4,3},{5,4},{6,5},{7,6},{8,7},{9,8},{10,9},{11,1... | collective-permute-start | bytes 52232 | tf_op jit(solution)/shard_map/ppermute | solution.py:17
  15.5 7.9 %copy-start = (f32[32,32,128]{2,1,0:T(8,128)S(1)}, f32[32,32,128]{2,1,0:T(8,128)}, u32[]{:S(2)}) copy-start(f32[32,32,128]{2,1,0:T(8,128)} %param.8) | copy-start | bytes 1572868
  15.5 7.9 %collective-permute-start.3 = (f32[34,1,128]{2,1,0:T(1,128)S(1)}, f32[34,1,128]{2,1,0:T(1,128)S(1)}, u32[]{:S(2)}, u32[]{:S(2)}) collective-permute-start(f32[34,1,128]{2,1,0:T(1,128)S(1)} %get-tuple-element.249), channel_id=1, source_target_pairs={{0,1},{1,2},{2,3},{3,4},{4,5},{5,6},{6,7},{7,8},{8,9},{9,10},{10,1... | collective-permute-start | bytes 52232 | tf_op jit(solution)/shard_map/ppermute | solution.py:14
  24.0 5.7 %collective-permute-start.4 = (f32[1,32,128]{2,1,0:T(8,128)S(1)}, f32[1,32,128]{2,1,0:T(8,128)S(1)}, u32[]{:S(2)}, u32[]{:S(2)}) collective-permute-start(f32[1,32,128]{2,1,0:T(8,128)S(1)} %get-tuple-element.261), channel_id=1, source_target_pairs={{64,0},{128,64},{192,128},{256,192},{320,256},{384,320},{448,384},... | collective-permute-start | bytes 49160 | tf_op jit(solution)/shard_map/ppermute | solution.py:17
  25.9 6.3 %collective-permute-start.5 = (f32[1,32,128]{2,1,0:T(8,128)S(1)}, f32[1,32,128]{2,1,0:T(8,128)S(1)}, u32[]{:S(2)}, u32[]{:S(2)}) collective-permute-start(f32[1,32,128]{2,1,0:T(8,128)S(1)} %get-tuple-element.260), channel_id=1, source_target_pairs={{0,64},{64,128},{128,192},{192,256},{256,320},{320,384},{384,448},... | collective-permute-start | bytes 49160 | tf_op jit(solution)/shard_map/ppermute | solution.py:14
  32.2 6.1 %collective-permute-start.6 = (f32[34,1,128]{2,1,0:T(1,128)S(1)}, f32[34,1,128]{2,1,0:T(1,128)S(1)}, u32[]{:S(2)}, u32[]{:S(2)}) collective-permute-start(f32[34,1,128]{2,1,0:T(1,128)S(1)} %get-tuple-element.246), channel_id=1, source_target_pairs={{1,0},{2,1},{3,2},{4,3},{5,4},{6,5},{7,6},{8,7},{9,8},{10,9},{11,1... | collective-permute-start | bytes 52232 | tf_op jit(solution)/shard_map/ppermute | solution.py:17
  34.2 7.8 %collective-permute-start.7 = (f32[34,1,128]{2,1,0:T(1,128)S(1)}, f32[34,1,128]{2,1,0:T(1,128)S(1)}, u32[]{:S(2)}, u32[]{:S(2)}) collective-permute-start(f32[34,1,128]{2,1,0:T(1,128)S(1)} %get-tuple-element.247), channel_id=1, source_target_pairs={{0,1},{1,2},{2,3},{3,4},{4,5},{5,6},{6,7},{7,8},{8,9},{9,10},{10,1... | collective-permute-start | bytes 52232 | tf_op jit(solution)/shard_map/ppermute | solution.py:14
  391.4 4.3 %collective-permute-start.8 = (f32[1,32,128]{2,1,0:T(8,128)S(1)}, f32[1,32,128]{2,1,0:T(8,128)S(1)}, u32[]{:S(2)}, u32[]{:S(2)}) collective-permute-start(f32[1,32,128]{2,1,0:T(8,128)S(1)} %get-tuple-element.257), channel_id=1, source_target_pairs={{64,0},{128,64},{192,128},{256,192},{320,256},{384,320},{448,384},... | collective-permute-start | bytes 49160 | tf_op jit(solution)/shard_map/ppermute | solution.py:17
  393.3 6.3 %collective-permute-start.9 = (f32[1,32,128]{2,1,0:T(8,128)S(1)}, f32[1,32,128]{2,1,0:T(8,128)S(1)}, u32[]{:S(2)}, u32[]{:S(2)}) collective-permute-start(f32[1,32,128]{2,1,0:T(8,128)S(1)} %get-tuple-element.256), channel_id=1, source_target_pairs={{0,64},{64,128},{128,192},{192,256},{256,320},{320,384},{384,448},... | collective-permute-start | bytes 49160 | tf_op jit(solution)/shard_map/ppermute | solution.py:14
  399.6 6.1 %collective-permute-start.10 = (f32[34,1,128]{2,1,0:T(1,128)S(1)}, f32[34,1,128]{2,1,0:T(1,128)S(1)}, u32[]{:S(2)}, u32[]{:S(2)}) collective-permute-start(f32[34,1,128]{2,1,0:T(1,128)S(1)} %get-tuple-element.244), channel_id=1, source_target_pairs={{1,0},{2,1},{3,2},{4,3},{5,4},{6,5},{7,6},{8,7},{9,8},{10,9},{11,1... | collective-permute-start | bytes 52232 | tf_op jit(solution)/shard_map/ppermute | solution.py:17
  403.0 7.8 %collective-permute-start.11 = (f32[34,1,128]{2,1,0:T(1,128)S(1)}, f32[34,1,128]{2,1,0:T(1,128)S(1)}, u32[]{:S(2)}, u32[]{:S(2)}) collective-permute-start(f32[34,1,128]{2,1,0:T(1,128)S(1)} %get-tuple-element.245), channel_id=1, source_target_pairs={{0,1},{1,2},{2,3},{3,4},{4,5},{5,6},{6,7},{7,8},{8,9},{9,10},{10,1... | collective-permute-start | bytes 52232 | tf_op jit(solution)/shard_map/ppermute | solution.py:14
  411.3 4.3 %collective-permute-start.12 = (f32[1,32,128]{2,1,0:T(8,128)S(1)}, f32[1,32,128]{2,1,0:T(8,128)S(1)}, u32[]{:S(2)}, u32[]{:S(2)}) collective-permute-start(f32[1,32,128]{2,1,0:T(8,128)S(1)} %get-tuple-element.253), channel_id=1, source_target_pairs={{64,0},{128,64},{192,128},{256,192},{320,256},{384,320},{448,384},... | collective-permute-start | bytes 49160 | tf_op jit(solution)/shard_map/ppermute | solution.py:17
  413.2 6.3 %collective-permute-start.13 = (f32[1,32,128]{2,1,0:T(8,128)S(1)}, f32[1,32,128]{2,1,0:T(8,128)S(1)}, u32[]{:S(2)}, u32[]{:S(2)}) collective-permute-start(f32[1,32,128]{2,1,0:T(8,128)S(1)} %get-tuple-element.252), channel_id=1, source_target_pairs={{0,64},{64,128},{128,192},{192,256},{256,320},{320,384},{384,448},... | collective-permute-start | bytes 49160 | tf_op jit(solution)/shard_map/ppermute | solution.py:14
  419.5 6.1 %collective-permute-start.14 = (f32[34,1,128]{2,1,0:T(1,128)S(1)}, f32[34,1,128]{2,1,0:T(1,128)S(1)}, u32[]{:S(2)}, u32[]{:S(2)}) collective-permute-start(f32[34,1,128]{2,1,0:T(1,128)S(1)} %get-tuple-element.242), channel_id=1, source_target_pairs={{1,0},{2,1},{3,2},{4,3},{5,4},{6,5},{7,6},{8,7},{9,8},{10,9},{11,1... | collective-permute-start | bytes 52232 | tf_op jit(solution)/shard_map/ppermute | solution.py:17
  421.5 7.8 %collective-permute-start.15 = (f32[34,1,128]{2,1,0:T(1,128)S(1)}, f32[34,1,128]{2,1,0:T(1,128)S(1)}, u32[]{:S(2)}, u32[]{:S(2)}) collective-permute-start(f32[34,1,128]{2,1,0:T(1,128)S(1)} %get-tuple-element.243), channel_id=1, source_target_pairs={{0,1},{1,2},{2,3},{3,4},{4,5},{5,6},{6,7},{7,8},{8,9},{9,10},{10,1... | collective-permute-start | bytes 52232 | tf_op jit(solution)/shard_map/ppermute | solution.py:14
where the time goes:
time: 431 us
  other arithmetic  204 us (47%)
  blocking collectives  132 us (31%)
  starting transfers between devices  40.8 us (9%)
  waiting for transfers between devices  31.7 us (7%)
  matrix products  11.9 us (3%)
  local copies, waits for them, and re-layouts  6.97 us (2%)
    unnamed x1, blocking collectives  132 us
    another operation x48, other arithmetic, forward(): factor = jnp.linalg.cholesky(block)  104 us
    another operation x32, other arithmetic, forward(): lax.linalg.triangular_solve(factor, half, left_side=True, lower=True, tra...  88.8 us
    ppermute x8, waiting for transfers between devices, with_halo(): lax.ppermute(lax.slice_in_dim(block, block.shape[dim] - width, None, axis...  31.7 us
    ppermute x8, starting transfers between devices, with_halo(): lax.ppermute(lax.slice_in_dim(block, block.shape[dim] - width, None, axis...  22.2 us
    ppermute x8, starting transfers between devices, with_halo(): lax.ppermute(lax.slice_in_dim(block, 0, width, axis=dim), axis, backward)  18.6 us
  transfers between devices with their start and end apart: 16, of which 8 were waited for; matrix products, arithmetic and copies ran while one was open for 0% of the time, Pallas kernels for 0%

commit v1 on v0

v1 whole, which is shorter than its diff:
```python
import math
import functools
import jax
import jax.numpy as jnp
from jax import lax
from jax.experimental import pallas as pl
from jax.experimental.pallas import tpu as pltpu
from jax.sharding import PartitionSpec as P

f32 = jnp.float32
MESH = pl.DeviceIdType.MESH
ROWS = 1024
PAD = 32
CHUNK = 256
NW, NN = 16, 64

RHO = 32.0 * (2.0 * math.cos(math.pi / 17) + 2.0 * math.cos(math.pi / 65)) / 128.0199
HALF = 1.0 - RHO * RHO / 2.0
RHO2 = RHO * RHO / 2.0 / HALF
ROOT = math.sqrt(1.0 - RHO2 * RHO2)
SIG = (1.0 - ROOT) / RHO2
SCALE = 2.0 / (HALF * ROOT)
TRIPS = 16


def iota(shape, dim):
    return lax.broadcasted_iota(jnp.int32, shape, dim)


def layer(ref, side, base=0):
    if side == 0:
        return ref[pl.ds(base, 32), :]
    if side == 1:
        return ref[pl.ds(base + ROWS - 32, 32), :]
    return ref[pl.ds(base + (0 if side == 2 else 31), 32, stride=32), :]


def add_layer(ref, side, value, base=0):
    if side == 0:
        ref[pl.ds(base, 32), :] = ref[pl.ds(base, 32), :] + value
    elif side == 1:
        at = base + ROWS - 32
        ref[pl.ds(at, 32), :] = ref[pl.ds(at, 32), :] + value
    else:
        at = base + (0 if side == 2 else 31)
        ref[pl.ds(at, 32, stride=32), :] = ref[pl.ds(at, 32, stride=32), :] + value


CORNERS = ((0, 2), (0, 3), (1, 2), (1, 3))
CORNER_ROW = (0, 31, ROWS - 32, ROWS - 1)


def coarse_factor(d_ref, w0, n0):
    lane, sub = iota((8, 128), 1), iota((8, 128), 0)
    z, r = lane // 8, lane % 8
    q = {}
    for c in range(4):
        for p in range(2):
            q[c, p] = 32.0 / (128.0 + d_ref[pl.ds(8 * p + c, 8, stride=16), :])

    def shifted(v, cols):
        if cols == 0:
            return v
        rolled = pltpu.roll(v, (-8 * cols) % 128, 1)
        inside = (z + cols >= 0) & (z + cols < 16)
        return jnp.where(inside, rolled, 0.0)

    for c in list(range(-8, 0)) + list(range(4, 12)):
        for p in range(2):
            q[c, p] = shifted(q[c % 4, p], c // 4)

    def gather(x, c, p):
        other = x[c, 1 - p]
        if p == 0:
            near = jnp.where(sub == 0, 0.0, pltpu.roll(other, 1, 0))
        else:
            near = jnp.where(sub == 7, 0.0, pltpu.roll(other, 7, 0))
        return (x[c - 1, p] + x[c + 1, p]) + (other + near)

    dw = jnp.where(r == 0, -1, jnp.where(r == 1, 1, jnp.where(r < 4, 0, jnp.where(r < 6, -1, 1))))
    dn = jnp.where(r < 2, 0, jnp.where(r == 2, -1, jnp.where(r == 3, 1, jnp.where(r % 2 == 0, -1, 1))))
    want_w, want_n = w0 + dw, n0 + dn - 4 * z

    def unit(c, p):
        hit = (2 * sub + p == want_w) & (want_n == c)
        return jnp.where(hit, q[c, p] * (1.0 / 32.0), 0.0)

    def color(c, which):
        return (c + which) % 2

    b = {}
    for c in range(-1, 5):
        b[c, color(c, 1)] = unit(c, color(c, 1))
    g = {}
    for c in range(4):
        p = color(c, 0)
        g[c] = unit(c, p) + q[c, p] * gather(b, c, p)

    c_two, c_cur, c_old = 4.0 * SIG / (RHO * RHO), 2.0 * SIG, SIG * SIG

    def trip(it, carry):
        acc, cur, old = carry
        x, o = {}, {}
        for c in range(-8, 12):
            x[c, color(c, 0)] = shifted(cur[c % 4], c // 4)
            if -6 <= c < 10:
                o[c] = shifted(old[c % 4], c // 4)
        acc = list(acc)
        first = jnp.where(it == 0, 0.5, 1.0).astype(f32)
        for app in range(4):
            lo, hi = -8 + 2 * app, 12 - 2 * app
            y = {}
            for c in range(lo + 1, hi - 1):
                p = color(c, 1)
                y[c, p] = q[c, p] * gather(x, c, p)
            new = {}
            for c in range(lo + 2, hi - 2):
                p = color(c, 0)
                t = (c_two * q[c, p]) * gather(y, c, p) - c_cur * x[c, p]
                if app == 0:
                    t = first * t
                new[c, p] = t - c_old * o[c]
            o = {c: x[c, color(c, 0)] for c in range(lo + 2, hi - 2)}
            x = new
            for c in range(4):
                acc[c] = acc[c] + x[c, color(c, 0)]
        return tuple(acc), tuple(x[c, color(c, 0)] for c in range(4)), tuple(o[c] for c in range(4))

    g = tuple(g[c] for c in range(4))
    zero = jnp.zeros((8, 128), f32)
    acc, _, _ = lax.fori_loop(0, TRIPS, trip, (tuple(0.5 * v for v in g), g, (zero,) * 4))
    x = {(c, color(c, 0)): SCALE * acc[c] for c in range(4)}
    x[-1, color(-1, 0)] = shifted(x[3, color(3, 0)], -1)
    x[4, color(4, 0)] = shifted(x[0, color(0, 0)], 1)
    out = {}
    for c in range(4):
        out[c, color(c, 0)] = x[c, color(c, 0)]
        p = color(c, 1)
        out[c, p] = b[c, p] + q[c, p] * gather(x, c, p)
    return out


def kernel(
    f_ref, cls_ref, drag_ref, depth_ref, out_ref,
    r_ref, s_ref, v0_ref, v1_ref,
    row, ga1, ga2, gb1, gb2, snd_a, rcv_a, snd_b, rcv_b, dsnd, drcv,
    gs, gr, hs, hr, ds, dr,
):
    w0, n0 = lax.axis_index("wide"), lax.axis_index("narrow")
    z0, x0 = n0 // 4, n0 % 4

    bar = pltpu.get_barrier_semaphore()

    def greet_narrow(p, _):
        pl.semaphore_signal(bar, inc=1, device_id=(w0, (n0 + p) % NN), device_id_type=MESH)
        return 0

    def greet_wide(p, _):
        pl.semaphore_signal(bar, inc=1, device_id=((w0 + p) % NW, n0), device_id_type=MESH)
        return 0

    sides = (
        ((w0 + NW - 1) % NW, n0),
        ((w0 + 1) % NW, n0),
        (w0, (n0 + NN - 1) % NN),
        (w0, (n0 + 1) % NN),
    )
    diags = tuple((sides[a][0], sides[b][1]) for a, b in CORNERS)
    for t in diags:
        pl.semaphore_signal(bar, inc=1, device_id=t, device_id_type=MESH)
    lax.fori_loop(1, NN, greet_narrow, 0)
    lax.fori_loop(1, NW, greet_wide, 0)

    exist = (w0 > 0, w0 < NW - 1, n0 > 0, n0 < NN - 1)

    lane = iota((1, 128), 1)
    depth = depth_ref[...]
    link = jnp.where(lane == 127, 0.0, 2.0 / (depth + pltpu.roll(depth, 127, 1)))
    up, down = link, pltpu.roll(link, 1, 1)
    ztotal = jnp.sum(depth, axis=1, keepdims=True)
    drags = [drag_ref[c] for c in range(4)]
    tables = [0.8 / (depth * (4.0 + d) + up + down) for d in drags]

    kinds = cls_ref[...]
    s2d = jnp.where(kinds == 0, drags[0], jnp.where(kinds == 1, drags[1], jnp.where(kinds == 2, drags[2], drags[3])))
    own_drag = jnp.sum(jnp.sum(s2d, axis=0, keepdims=True), axis=1, keepdims=True) * (1.0 / ROWS)
    row[0:1, :] = jnp.broadcast_to(own_drag, (1, 128))

    pl.semaphore_wait(bar, (NN - 1) + (NW - 1) + 4)

    sub16, lane16 = iota((16, 128), 0), iota((16, 128), 1)
    mine = x0 * 16 + z0

    def gather_start(k, buf):
        def send(p, _):
            pltpu.make_async_remote_copy(
                src_ref=row.at[pl.ds(8 * k, 1)], dst_ref=buf.at[pl.ds(mine, 1)], send_sem=gs.at[2 * k],
                recv_sem=gr.at[2 * k], device_id=(w0, (n0 + p) % NN), device_id_type=MESH,
            ).start()
            return 0

        lax.fori_loop(1, NN, send, 0)
        buf[pl.ds(mine, 1), :] = row[8 * k : 8 * k + 1, :]

    def drain(buf, rows, sem):
        pltpu.make_async_copy(buf.at[pl.ds(0, rows)], buf.at[pl.ds(0, rows)], sem).wait()

    def gather_middle(k, buf, buf2):
        drain(buf, NN - 1, gr.at[2 * k])
        at = pl.multiple_of(w0 * 8, 8)
        rows = [
            jnp.sum(jnp.where(lane16 // 8 == sub16, buf[16 * x : 16 * x + 16, :], 0.0), axis=0, keepdims=True)
            for x in range(4)
        ]
        buf2[pl.ds(at, 8), :] = jnp.concatenate(rows + rows, axis=0)

        def send(p, _):
            pltpu.make_async_remote_copy(
                src_ref=buf2.at[pl.ds(at, 8)], dst_ref=buf2.at[pl.ds(at, 8)], send_sem=gs.at[2 * k + 1],
                recv_sem=gr.at[2 * k + 1], device_id=((w0 + p) % NW, n0), device_id_type=MESH,
            ).start()
            return 0

        lax.fori_loop(1, NW, send, 0)

    def gather_end(k, buf2):
        drain(buf2, 8 * (NW - 1), gr.at[2 * k + 1])

    def gather_close(k, buf, buf2):
        drain(buf, NN - 1, gs.at[2 * k])
        drain(buf2, 8 * (NW - 1), gs.at[2 * k + 1])

    gather_start(0, ga1)

    cf = kinds.astype(f32)
    eye = jnp.where(iota((32, 32), 0) == iota((32, 32), 1), 1.0, 0.0).astype(f32)
    ones = jnp.ones((32, 128), f32)
    zpad = jnp.zeros((PAD, 128), f32)
    for ref in (v0_ref, v1_ref):
        ref[0:PAD, :] = zpad
        ref[PAD + ROWS : PAD + ROWS + PAD, :] = zpad
    sum_f = jnp.zeros((8, 128), f32)
    for k in range(ROWS // CHUNK):
        ni = CHUNK // 32
        spread = (cf[k * ni : (k + 1) * ni][:, None, :] * eye[None]).reshape(CHUNK, 32)
        kind = jnp.dot(spread, ones, preferred_element_type=f32)
        is0, is1, is2 = kind < 0.5, kind < 1.5, kind < 2.5
        rr = jnp.where(is0, tables[0], jnp.where(is1, tables[1], jnp.where(is2, tables[2], tables[3])))
        ss = jnp.where(is0, drags[0], jnp.where(is1, drags[1], jnp.where(is2, drags[2], drags[3])))
        f = f_ref[k * CHUNK : (k + 1) * CHUNK, :]
        r_ref[k * CHUNK : (k + 1) * CHUNK, :] = rr
        s_ref[k * CHUNK : (k + 1) * CHUNK, :] = ss
        v0_ref[PAD + k * CHUNK : PAD + (k + 1) * CHUNK, :] = rr * f
        sum_f = sum_f + jnp.sum(f.reshape(CHUNK // 8, 8, 128), axis=0)

    jpos = iota((CHUNK, 128), 0) % 32

    def sweep(src, k):
        lo = k * CHUNK
        c = src[PAD + lo : PAD + lo + CHUNK, :]
        near = src[lo : lo + CHUNK, :] + src[2 * PAD + lo : 2 * PAD + lo + CHUNK, :]
        near = near + jnp.where(jpos == 0, 0.0, src[PAD + lo - 1 : PAD + lo - 1 + CHUNK, :])
        near = near + jnp.where(jpos == 31, 0.0, src[PAD + lo + 1 : PAD + lo + 1 + CHUNK, :])
        vert = up * pltpu.roll(c, 127, 1) + down * pltpu.roll(c, 1, 1)
        rr, f = r_ref[lo : lo + CHUNK, :], f_ref[lo : lo + CHUNK, :]
        return 0.2 * c + rr * (f + (depth * near + vert))

    sum_s = jnp.zeros((8, 128), f32)
    for k in range(ROWS // CHUNK):
        lo = k * CHUNK
        v = sweep(v0_ref, k)
        v1_ref[PAD + lo : PAD + lo + CHUNK, :] = v
        sum_s = sum_s + jnp.sum((s_ref[lo : lo + CHUNK, :] * v).reshape(CHUNK // 8, 8, 128), axis=0)

    def exchange(snd, rcv, base, corner_src):
        copies = []
        for side, t in enumerate(sides):
            copies.append(
                pltpu.make_async_remote_copy(
                    src_ref=snd.at[side], dst_ref=rcv.at[side ^ 1], send_sem=hs.at[base + side],
                    recv_sem=hr.at[base + (side ^ 1)], device_id=t, device_id_type=MESH,
                )
            )
        for corner, t in enumerate(diags):
            slot = base // 4
            dsnd[slot, corner, 0:1, :] = corner_src[PAD + CORNER_ROW[corner] : PAD + CORNER_ROW[corner] + 1, :]
            copies.append(
                pltpu.make_async_remote_copy(
                    src_ref=dsnd.at[slot, corner], dst_ref=drcv.at[slot, 3 - corner], send_sem=ds.at[base + corner],
                    recv_sem=dr.at[base + 3 - corner], device_id=t, device_id_type=MESH,
                )
            )
        for c in copies:
            c.start()
        return copies

    edge_sum = jnp.zeros((1, 128), f32)
    for side in range(4):
        snd_a[side, 0:32, :] = layer(v0_ref, side, PAD)
        snd_a[side, 32:64, :] = layer(r_ref, side)
        total = jnp.sum(layer(v1_ref, side, PAD), axis=0, keepdims=True)
        edge_sum = edge_sum + total
        snd_a[side, 64:72, :] = jnp.broadcast_to(total, (8, 128))
    sent_a = exchange(snd_a, rcv_a, 0, v0_ref)

    gather_middle(0, ga1, ga2)

    for c in sent_a:
        c.wait_recv()
    present = [jnp.where(e, 1.0, 0.0).astype(f32) for e in exist]
    r_out = [rcv_a[side, 32:64, :] * present[side] for side in range(4)]
    w_out = [depth * r_out[side] for side in range(4)]
    w_in = [depth * layer(r_ref, side) for side in range(4)]
    sub32 = iota((32, 128), 0)
    ends = jnp.where((sub32 == 0) | (sub32 == 31), 2.0, 1.0)
    flux = sum_s_row = jnp.sum(sum_s, axis=0, keepdims=True) + edge_sum
    deltas = []
    for side in range(4):
        delta = w_in[side] * (rcv_a[side, 0:32, :] * present[side])
        deltas.append(delta)
        term = (layer(s_ref, side) + ends) * delta - w_out[side] * layer(v0_ref, side, PAD)
        flux = flux + jnp.sum(term, axis=0, keepdims=True) - rcv_a[side, 64:65, :] * present[side]
    corner_first = []
    for corner, (a, b) in enumerate(CORNERS):
        at_a, at_b = 31 * (b - 2), 31 * a
        both = present[a] * present[b]
        value = drcv[0, corner, 0:1, :] * both
        flux = flux - (w_out[a][at_a : at_a + 1] + w_out[b][at_b : at_b + 1]) * value
    res = jnp.sum(sum_f, axis=0, keepdims=True) - depth * flux
    own_res = jnp.sum(res, axis=1, keepdims=True)
    row[8:9, :] = jnp.broadcast_to(own_res, (1, 128))
    gather_start(1, gb1)

    for side in range(4):
        add_layer(v1_ref, side, deltas[side], PAD)
    for k in range(ROWS // CHUNK):
        v0_ref[PAD + k * CHUNK : PAD + (k + 1) * CHUNK, :] = sweep(v1_ref, k)
    for side in range(4):
        snd_b[side, 0:32, :] = layer(v1_ref, side, PAD)
        snd_b[side, 32:64, :] = layer(v0_ref, side, PAD)
    sent_b = exchange(snd_b, rcv_b, 4, v1_ref)

    gather_end(0, ga2)
    columns = coarse_factor(ga2, w0, n0)
    gather_middle(1, gb1, gb2)

    for c in sent_b:
        c.wait_recv()
    outside = []
    for side in range(4):
        add_layer(v0_ref, side, w_in[side] * (rcv_b[side, 0:32, :] * present[side]), PAD)
        third = rcv_b[side, 32:64, :] * present[side] + w_out[side] * layer(v1_ref, side, PAD)
        outside.append(third)
    tips = []
    for side in range(4):
        lo_corner = (0, 2, 0, 1)[side]
        hi_corner = (1, 3, 2, 3)[side]
        pair = []
        for corner in (lo_corner, hi_corner):
            a, b = CORNERS[corner]
            pair.append(drcv[1, corner, 0:1, :] * (present[a] * present[b]))
        tip = jnp.where(sub32 == 0, pair[0], jnp.where(sub32 == 31, pair[1], 0.0))
        outside[side] = outside[side] + w_out[side] * tip

    gather_end(1, gb2)
    total = jnp.zeros((8, 128), f32)
    for c in range(4):
        for p in range(2):
            total = total + columns[c, p] * gb2[pl.ds(8 * p + c, 8, stride=16), :]
    line = jnp.sum(total, axis=0, keepdims=True)
    line = jnp.where(iota((8, 128), 1) % 8 == iota((8, 128), 0), line, 0.0)
    near = jnp.sum(line, axis=1, keepdims=True) / ztotal
    near = jnp.broadcast_to(near, (8, 128))
    e = [near[k : k + 1, :] for k in range(8)]
    e0 = (own_res / ztotal + 32.0 * (e[0] + e[1] + e[2] + e[3])) / (128.0 + own_drag)
    level = 4.0 * depth + up + down
    for side in range(4):
        add_layer(v0_ref, side, w_in[side] * (e[side] - e0), PAD)
        lo_corner = (0, 2, 0, 1)[side]
        hi_corner = (1, 3, 2, 3)[side]
        jump = jnp.where(
            sub32 == 0, e[4 + lo_corner] - e[side], jnp.where(sub32 == 31, e[4 + hi_corner] - e[side], 0.0)
        )
        own = (0.2 * present[side] + r_out[side] * level) * e[side]
        outside[side] = outside[side] + own + w_out[side] * ((e0 - e[side]) + jump)
    for k in range(ROWS // CHUNK):
        lo = k * CHUNK
        v1_ref[PAD + lo : PAD + lo + CHUNK, :] = v0_ref[PAD + lo : PAD + lo + CHUNK, :] + (
            0.2 + r_ref[lo : lo + CHUNK, :] * level
        ) * e0
    for k in range(ROWS // CHUNK):
        lo = k * CHUNK
        out_ref[lo : lo + CHUNK, :] = sweep(v1_ref, k)
    for side in range(4):
        add_layer(out_ref, side, w_in[side] * outside[side])

    for c in sent_a + sent_b:
        c.wait_send()
    gather_close(0, ga1, ga2)
    gather_close(1, gb1, gb2)


def local(forcing, classes, drag, depth):
    vmem, smem = pl.BlockSpec(memory_space=pltpu.VMEM), pl.BlockSpec(memory_space=pltpu.SMEM)
    field = pltpu.VMEM((ROWS, 128), f32)
    padded = pltpu.VMEM((ROWS + 2 * PAD, 128), f32)
    out = pl.pallas_call(
        kernel,
        out_shape=jax.ShapeDtypeStruct((ROWS, 128), f32),
        in_specs=[vmem, vmem, smem, vmem],
        out_specs=vmem,
        scratch_shapes=[
            field, field, padded, padded,
            pltpu.VMEM((16, 128), f32),
            pltpu.VMEM((NN, 128), f32), pltpu.VMEM((8 * NW, 128), f32),
            pltpu.VMEM((NN, 128), f32), pltpu.VMEM((8 * NW, 128), f32),
            pltpu.VMEM((4, 72, 128), f32), pltpu.VMEM((4, 72, 128), f32),
            pltpu.VMEM((4, 64, 128), f32), pltpu.VMEM((4, 64, 128), f32),
            pltpu.VMEM((2, 4, 8, 128), f32), pltpu.VMEM((2, 4, 8, 128), f32),
            pltpu.SemaphoreType.DMA((4,)), pltpu.SemaphoreType.DMA((4,)),
            pltpu.SemaphoreType.DMA((8,)), pltpu.SemaphoreType.DMA((8,)),
            pltpu.SemaphoreType.DMA((8,)), pltpu.SemaphoreType.DMA((8,)),
        ],
        compiler_params=pltpu.CompilerParams(
            collective_id=0, has_side_effects=True, vmem_limit_bytes=40 * 1024 * 1024
        ),
        name="vcycle",
    )(forcing.reshape(ROWS, 128), classes, drag, depth.reshape(1, 128))
    return out.reshape(forcing.shape)


def solution(mesh):
    in_specs = (P("wide", "narrow", None), P("wide", "narrow"), P(), P())
    out_specs = P("wide", "narrow", None)
    return jax.shard_map(local, mesh=mesh, in_specs=in_specs, out_specs=out_specs, check_vma=False)
```

time: 431 us -> 53.2 us (0.12)
  the two profiles are of different devices: /device:TPU:96 before, /device:TPU:1 now
where the time goes in v1:
time: 53.2 us; the launch traced here: 53 us
  Pallas kernels  49.7 us (93%)
  local copies, waits for them, and re-layouts  3.22 us (6%)
    pallas_call x1, Pallas kernels, local(): pl.pallas_call(kernel, out_shape=jax.ShapeDtypeStruct((ROWS, 128), f32),...  49.7 us
    unnamed x9, local copies, waits for them, and re-layouts  3.22 us

profile of v1, /device:TPU:1, one launch (start us, length us, event | category | flops | bytes accessed | tf_op | source)
XLA Modules:
  0.0 53.0 jit_solution(7619758361533251820)
XLA Ops:
  0.0 0.0 copy-start.2
  0.0 0.0 copy-start.3
  0.0 0.7 %copy-done.2 = f32[4]{0:T(128)S(1)} copy-done((f32[4]{0:T(128)S(1)}, f32[4]{0:T(128)}, u32[]{:S(2)}) %copy-start.2) | copy-done | bytes 40
  0.7 0.0 copy-done.3
  0.7 0.0 copy-start
  0.7 1.0 %copy-done = f32[32,32,128]{2,1,0:T(8,128)S(1)} copy-done((f32[32,32,128]{2,1,0:T(8,128)S(1)}, f32[32,32,128]{2,1,0:T(8,128)}, u32[]{:S(2)}) %copy-start) | copy-done | bytes 524312
  1.7 0.0 copy-start.1
  1.7 0.7 %copy-done.1 = s32[32,32]{1,0:T(8,128)S(1)} copy-done((s32[32,32]{1,0:T(8,128)S(1)}, s32[32,32]{1,0:T(8,128)}, u32[]{:S(2)}) %copy-start.1) | copy-done | bytes 4120
  2.4 49.7 %vcycle.1 = f32[1024,128]{1,0:T(8,128)S(1)} custom-call(f32[1024,128]{1,0:T(8,128)S(1)} %bitcast.4, s32[32,32]{1,0:T(8,128)S(1)} %copy-done.1, f32[4]{0:T(128)S(1)} %copy-done.2, f32[1,128]{1,0:T(1,128)S(1)} %bitcast.5), custom_call_target="tpu_custom_call" | custom-call | tf_op jit(solution)/shard_map/vcycle/pallas_call | solution.py:407
  52.2 0.8 %copy.6 = f32[32,32,128]{2,1,0:T(8,128)} copy(f32[32,32,128]{2,1,0:T(8,128)S(1)} %bitcast.3) | data formatting | bytes 1048576
Async XLA Ops:
  0.0 0.7 %copy-start.2 = (f32[4]{0:T(128)S(1)}, f32[4]{0:T(128)}, u32[]{:S(2)}) copy-start(f32[4]{0:T(128)} %drag_ref.1) | copy-start | bytes 52
  0.0 0.7 %copy-start.3 = (f32[128]{0:T(128)S(1)}, f32[128]{0:T(128)}, u32[]{:S(2)}) copy-start(f32[128]{0:T(128)} %param.7) | copy-start | bytes 1540
  0.7 1.0 %copy-start = (f32[32,32,128]{2,1,0:T(8,128)S(1)}, f32[32,32,128]{2,1,0:T(8,128)}, u32[]{:S(2)}) copy-start(f32[32,32,128]{2,1,0:T(8,128)} %param.4) | copy-start | bytes 1572868
  1.7 0.7 %copy-start.1 = (s32[32,32]{1,0:T(8,128)S(1)}, s32[32,32]{1,0:T(8,128)}, u32[]{:S(2)}) copy-start(s32[32,32]{1,0:T(8,128)} %cls_ref.1) | copy-start | bytes 12292

commit v2 on v1

v2 whole, which is shorter than its diff:
```python
import math
import functools
import jax
import jax.numpy as jnp
from jax import lax
from jax.experimental import pallas as pl
from jax.experimental.pallas import tpu as pltpu
from jax.sharding import PartitionSpec as P

f32 = jnp.float32
MESH = pl.DeviceIdType.MESH
ROWS = 1024
PAD = 32
CHUNK = 256
NW, NN = 16, 64

RHO = 32.0 * (2.0 * math.cos(math.pi / 17) + 2.0 * math.cos(math.pi / 65)) / 128.0199
HALF = 1.0 - RHO * RHO / 2.0
RHO2 = RHO * RHO / 2.0 / HALF
ROOT = math.sqrt(1.0 - RHO2 * RHO2)
SIG = (1.0 - ROOT) / RHO2
SCALE = 2.0 / (HALF * ROOT)
TRIPS = 16


def iota(shape, dim):
    return lax.broadcasted_iota(jnp.int32, shape, dim)


def layer(ref, side, base=0):
    if side == 0:
        return ref[pl.ds(base, 32), :]
    if side == 1:
        return ref[pl.ds(base + ROWS - 32, 32), :]
    return ref[pl.ds(base + (0 if side == 2 else 31), 32, stride=32), :]


def add_layer(ref, side, value, base=0):
    if side == 0:
        ref[pl.ds(base, 32), :] = ref[pl.ds(base, 32), :] + value
    elif side == 1:
        at = base + ROWS - 32
        ref[pl.ds(at, 32), :] = ref[pl.ds(at, 32), :] + value
    else:
        at = base + (0 if side == 2 else 31)
        ref[pl.ds(at, 32, stride=32), :] = ref[pl.ds(at, 32, stride=32), :] + value


CORNERS = ((0, 2), (0, 3), (1, 2), (1, 3))
CORNER_ROW = (0, 31, ROWS - 32, ROWS - 1)


def coarse_factor(d_ref, w0, n0):
    lane, sub = iota((8, 128), 1), iota((8, 128), 0)
    z, r = lane // 8, lane % 8
    q = {}
    for c in range(4):
        for p in range(2):
            q[c, p] = 32.0 / (128.0 + d_ref[pl.ds(8 * p + c, 8, stride=16), :])

    def shifted(v, cols):
        if cols == 0:
            return v
        rolled = pltpu.roll(v, (-8 * cols) % 128, 1)
        inside = (z + cols >= 0) & (z + cols < 16)
        return jnp.where(inside, rolled, 0.0)

    for c in list(range(-8, 0)) + list(range(4, 12)):
        for p in range(2):
            q[c, p] = shifted(q[c % 4, p], c // 4)

    def gather(x, c, p):
        other = x[c, 1 - p]
        if p == 0:
            near = jnp.where(sub == 0, 0.0, pltpu.roll(other, 1, 0))
        else:
            near = jnp.where(sub == 7, 0.0, pltpu.roll(other, 7, 0))
        return (x[c - 1, p] + x[c + 1, p]) + (other + near)

    dw = jnp.where(r == 0, -1, jnp.where(r == 1, 1, jnp.where(r < 4, 0, jnp.where(r < 6, -1, 1))))
    dn = jnp.where(r < 2, 0, jnp.where(r == 2, -1, jnp.where(r == 3, 1, jnp.where(r % 2 == 0, -1, 1))))
    want_w, want_n = w0 + dw, n0 + dn - 4 * z

    def unit(c, p):
        hit = (2 * sub + p == want_w) & (want_n == c)
        return jnp.where(hit, q[c, p] * (1.0 / 32.0), 0.0)

    def color(c, which):
        return (c + which) % 2

    b = {}
    for c in range(-1, 5):
        b[c, color(c, 1)] = unit(c, color(c, 1))
    g = {}
    for c in range(4):
        p = color(c, 0)
        g[c] = unit(c, p) + q[c, p] * gather(b, c, p)

    c_two, c_cur, c_old = 4.0 * SIG / (RHO * RHO), 2.0 * SIG, SIG * SIG

    def trip(it, carry):
        acc, cur, old = carry
        x, o = {}, {}
        for c in range(-8, 12):
            x[c, color(c, 0)] = shifted(cur[c % 4], c // 4)
            if -6 <= c < 10:
                o[c] = shifted(old[c % 4], c // 4)
        acc = list(acc)
        first = jnp.where(it == 0, 0.5, 1.0).astype(f32)
        for app in range(4):
            lo, hi = -8 + 2 * app, 12 - 2 * app
            y = {}
            for c in range(lo + 1, hi - 1):
                p = color(c, 1)
                y[c, p] = q[c, p] * gather(x, c, p)
            new = {}
            for c in range(lo + 2, hi - 2):
                p = color(c, 0)
                t = (c_two * q[c, p]) * gather(y, c, p) - c_cur * x[c, p]
                if app == 0:
                    t = first * t
                new[c, p] = t - c_old * o[c]
            o = {c: x[c, color(c, 0)] for c in range(lo + 2, hi - 2)}
            x = new
            for c in range(4):
                acc[c] = acc[c] + x[c, color(c, 0)]
        return tuple(acc), tuple(x[c, color(c, 0)] for c in range(4)), tuple(o[c] for c in range(4))

    g = tuple(g[c] for c in range(4))
    zero = jnp.zeros((8, 128), f32)
    acc, _, _ = lax.fori_loop(0, TRIPS, trip, (tuple(0.5 * v for v in g), g, (zero,) * 4))
    x = {(c, color(c, 0)): SCALE * acc[c] for c in range(4)}
    x[-1, color(-1, 0)] = shifted(x[3, color(3, 0)], -1)
    x[4, color(4, 0)] = shifted(x[0, color(0, 0)], 1)
    out = {}
    for c in range(4):
        out[c, color(c, 0)] = x[c, color(c, 0)]
        p = color(c, 1)
        out[c, p] = b[c, p] + q[c, p] * gather(x, c, p)
    return out


def kernel(
    f_hbm, cls_hbm, drag_hbm, depth_hbm, out_hbm,
    f_ref, cls_ref, drag_ref, depth_ref,
    r_ref, s_ref, v0_ref, v1_ref, base_ref, unit_ref,
    row, ga1, ga2, gb1, gb2, snd_a, rcv_a, snd_b, rcv_b, dsnd, drcv,
    load, gs, gr, hs, hr, ds, dr, credit, store,
):
    w0, n0 = lax.axis_index("wide"), lax.axis_index("narrow")
    z0, x0 = n0 // 4, n0 % 4

    loads = [
        pltpu.make_async_copy(src, dst, load.at[k])
        for k, (src, dst) in enumerate(
            ((cls_hbm, cls_ref), (drag_hbm, drag_ref), (depth_hbm, depth_ref), (f_hbm, f_ref))
        )
    ]
    for c in loads:
        c.start()

    bar = pltpu.get_barrier_semaphore()

    def greet(w, n):
        pl.semaphore_signal(bar, inc=1, device_id=(w, n), device_id_type=MESH)

    def beside_x(p):
        return z0 * 4 + (x0 + p) % 4

    sides = ((w0 - 1, n0), (w0 + 1, n0), (w0, n0 - 1), (w0, n0 + 1))
    exist = (w0 > 0, w0 < NW - 1, n0 > 0, n0 < NN - 1)
    diags = tuple((sides[a][0], sides[b][1]) for a, b in CORNERS)
    dexist = tuple(exist[a] & exist[b] for a, b in CORNERS)

    def greet_wide(p, _):
        greet((w0 + p) % NW, n0)
        return 0

    def greet_above(n, _):
        greet(w0, n)
        return 0

    for p in range(1, 4):
        greet(w0, beside_x(p))
    for t, there in zip(diags, dexist):
        pl.when(there)(functools.partial(greet, *t))
    pl.when((x0 == 0) & (z0 > 0))(functools.partial(greet, w0, n0 - 1))
    lax.fori_loop(1, NW, greet_wide, 0)
    lax.fori_loop(4 * z0 + 4, NN, greet_above, 0)

    for side in range(4):

        @pl.when(jnp.logical_not(exist[side]))
        def _(side=side):
            rcv_a[side] = jnp.zeros((72, 128), f32)
            rcv_b[side] = jnp.zeros((64, 128), f32)

    for corner in range(4):

        @pl.when(jnp.logical_not(dexist[corner]))
        def _(corner=corner):
            drcv[0, corner] = jnp.zeros((8, 128), f32)
            drcv[1, corner] = jnp.zeros((8, 128), f32)

    zpad = jnp.zeros((PAD, 128), f32)
    for ref in (v0_ref, v1_ref):
        ref[0:PAD, :] = zpad
        ref[PAD + ROWS : PAD + ROWS + PAD, :] = zpad

    for c in loads[:3]:
        c.wait()
    lane = iota((1, 128), 1)
    depth = depth_ref[...]
    link = jnp.where(lane == 127, 0.0, 2.0 / (depth + pltpu.roll(depth, 127, 1)))
    up, down = link, pltpu.roll(link, 1, 1)
    ztotal = jnp.sum(depth, axis=1, keepdims=True)
    drags = [drag_ref[c] for c in range(4)]
    tables = [0.8 / (depth * (4.0 + d) + up + down) for d in drags]

    kinds = cls_ref[...]

    cf = kinds.astype(f32)
    eye = jnp.where(iota((32, 32), 0) == iota((32, 32), 1), 1.0, 0.0).astype(f32)
    ones = jnp.ones((32, 128), f32)
    loads[3].wait()
    sum_f = jnp.zeros((8, 128), f32)
    for k in range(ROWS // CHUNK):
        ni = CHUNK // 32
        spread = (cf[k * ni : (k + 1) * ni][:, None, :] * eye[None]).reshape(CHUNK, 32)
        kind = jnp.dot(spread, ones, preferred_element_type=f32)
        is0, is1, is2 = kind < 0.5, kind < 1.5, kind < 2.5
        rr = jnp.where(is0, tables[0], jnp.where(is1, tables[1], jnp.where(is2, tables[2], tables[3])))
        ss = jnp.where(is0, drags[0], jnp.where(is1, drags[1], jnp.where(is2, drags[2], drags[3])))
        f = f_ref[k * CHUNK : (k + 1) * CHUNK, :]
        r_ref[k * CHUNK : (k + 1) * CHUNK, :] = rr
        s_ref[k * CHUNK : (k + 1) * CHUNK, :] = ss
        v0_ref[PAD + k * CHUNK : PAD + (k + 1) * CHUNK, :] = rr * f
        sum_f = sum_f + jnp.sum(f.reshape(CHUNK // 8, 8, 128), axis=0)

    def sweep(src, lo, n, forced=True):
        jpos = iota((n, 128), 0) % 32
        c = src[PAD + lo : PAD + lo + n, :]
        near = src[lo : lo + n, :] + src[2 * PAD + lo : 2 * PAD + lo + n, :]
        near = near + jnp.where(jpos == 0, 0.0, src[PAD + lo - 1 : PAD + lo - 1 + n, :])
        near = near + jnp.where(jpos == 31, 0.0, src[PAD + lo + 1 : PAD + lo + 1 + n, :])
        force = depth * near + (up * pltpu.roll(c, 127, 1) + down * pltpu.roll(c, 1, 1))
        if forced:
            force = f_ref[lo : lo + n, :] + force
        return 0.2 * c + r_ref[lo : lo + n, :] * force

    def sweep_column(src, side):
        at = 0 if side == 2 else 31
        c = src[pl.ds(PAD + at, 32, stride=32), :]
        near = src[pl.ds(at, 32, stride=32), :] + src[pl.ds(2 * PAD + at, 32, stride=32), :]
        near = near + src[pl.ds(PAD + (1 if side == 2 else 30), 32, stride=32), :]
        force = depth * near + (up * pltpu.roll(c, 127, 1) + down * pltpu.roll(c, 1, 1))
        return 0.2 * c + layer(r_ref, side) * (layer(f_ref, side) + force)

    def exchange(snd, rcv, base, corner_src):
        copies = []
        for side, t in enumerate(sides):
            copy = pltpu.make_async_remote_copy(
                src_ref=snd.at[side], dst_ref=rcv.at[side ^ 1], send_sem=hs.at[base + side],
                recv_sem=hr.at[base + (side ^ 1)], device_id=t, device_id_type=MESH,
            )
            mirror = pltpu.make_async_remote_copy(
                src_ref=snd.at[side], dst_ref=rcv.at[side], send_sem=hs.at[base + side],
                recv_sem=hr.at[base + side], device_id=t, device_id_type=MESH,
            )
            copies.append((exist[side], copy, mirror))
        for corner, t in enumerate(diags):
            slot = base // 4
            dsnd[slot, corner, 0:1, :] = corner_src[PAD + CORNER_ROW[corner] : PAD + CORNER_ROW[corner] + 1, :]
            copy = pltpu.make_async_remote_copy(
                src_ref=dsnd.at[slot, corner], dst_ref=drcv.at[slot, 3 - corner], send_sem=ds.at[base + corner],
                recv_sem=dr.at[base + 3 - corner], device_id=t, device_id_type=MESH,
            )
            mirror = pltpu.make_async_remote_copy(
                src_ref=dsnd.at[slot, corner], dst_ref=drcv.at[slot, corner], send_sem=ds.at[base + corner],
                recv_sem=dr.at[base + corner], device_id=t, device_id_type=MESH,
            )
            copies.append((dexist[corner], copy, mirror))
        for there, copy, _ in copies:
            pl.when(there)(copy.start)
        return copies

    def arrive(copies):
        for there, _, mirror in copies:
            pl.when(there)(mirror.wait_recv)

    edge_sum = jnp.zeros((1, 128), f32)
    for side in range(4):
        snd_a[side, 0:32, :] = layer(v0_ref, side, PAD)
        snd_a[side, 32:64, :] = layer(r_ref, side)
        swept = sweep(v0_ref, (0, ROWS - 32)[side], 32) if side < 2 else sweep_column(v0_ref, side)
        total = jnp.sum(swept, axis=0, keepdims=True)
        edge_sum = edge_sum + total
        snd_a[side, 64:72, :] = jnp.broadcast_to(total, (8, 128))

    hello = 4 * z0 + 3 + (NW - 1) + jnp.where((x0 == 3) & (z0 < 15), 1, 0)
    for there in dexist:
        hello = hello + jnp.where(there, 1, 0)
    pl.semaphore_wait(bar, hello)

    sub16, lane16 = iota((16, 128), 0), iota((16, 128), 1)
    mine = x0 * 16 + z0

    def drain(buf, rows, sem):
        pltpu.make_async_copy(buf.at[pl.ds(0, rows)], buf.at[pl.ds(0, rows)], sem).wait()

    def narrow_send(k, buf, n):
        pltpu.make_async_remote_copy(
            src_ref=row.at[pl.ds(8 * k, 1)], dst_ref=buf.at[pl.ds(mine, 1)], send_sem=gs.at[2 * k],
            recv_sem=gr.at[2 * k], device_id=(w0, n), device_id_type=MESH,
        ).start()

    def gather_start(k, buf):
        buf[pl.ds(mine, 1), :] = row[8 * k : 8 * k + 1, :]

        def send(n, _):
            narrow_send(k, buf, n)
            return 0

        lax.fori_loop(0, 4 * z0, send, 0)
        for p in range(1, 4):
            narrow_send(k, buf, beside_x(p))

    def gather_above():
        @pl.when(z0 < 15)
        def _():
            pl.semaphore_wait(credit, 4 * (15 - z0))


        def send(n, _):
            narrow_send(0, ga1, n)
            narrow_send(1, gb1, n)
            return 0

        lax.fori_loop(4 * z0 + 4, NN, send, 0)

    def gather_middle(k, buf, buf2):
        drain(buf, NN - 1, gr.at[2 * k])
        at = pl.multiple_of(w0 * 8, 8)
        rows = [
            jnp.sum(jnp.where(lane16 // 8 == sub16, buf[16 * x : 16 * x + 16, :], 0.0), axis=0, keepdims=True)
            for x in range(4)
        ]
        buf2[pl.ds(at, 8), :] = jnp.concatenate(rows + rows, axis=0)

        def send(p, _):
            pltpu.make_async_remote_copy(
                src_ref=buf2.at[pl.ds(at, 8)], dst_ref=buf2.at[pl.ds(at, 8)], send_sem=gs.at[2 * k + 1],
                recv_sem=gr.at[2 * k + 1], device_id=((w0 + p) % NW, n0), device_id_type=MESH,
            ).start()
            return 0

        lax.fori_loop(1, NW, send, 0)

    def gather_end(k, buf2):
        drain(buf2, 8 * (NW - 1), gr.at[2 * k + 1])

    def gather_close(k, buf, buf2):
        drain(buf, NN - 1, gs.at[2 * k])
        drain(buf2, 8 * (NW - 1), gs.at[2 * k + 1])

    sent_a = exchange(snd_a, rcv_a, 0, v0_ref)
    s2d = jnp.where(kinds == 0, drags[0], jnp.where(kinds == 1, drags[1], jnp.where(kinds == 2, drags[2], drags[3])))
    own_drag = jnp.sum(jnp.sum(s2d, axis=0, keepdims=True), axis=1, keepdims=True) * (1.0 / ROWS)
    row[0:1, :] = jnp.broadcast_to(own_drag, (1, 128))
    gather_start(0, ga1)

    def give_credit(n, _):
        pl.semaphore_signal(credit, inc=1, device_id=(w0, n), device_id_type=MESH)
        return 0

    lax.fori_loop(0, 4 * z0, give_credit, 0)

    sum_s = jnp.zeros((8, 128), f32)
    for k in range(ROWS // CHUNK):
        lo = k * CHUNK
        v = sweep(v0_ref, lo, CHUNK)
        v1_ref[PAD + lo : PAD + lo + CHUNK, :] = v
        sum_s = sum_s + jnp.sum((s_ref[lo : lo + CHUNK, :] * v).reshape(CHUNK // 8, 8, 128), axis=0)

    arrive(sent_a)
    r_out = [rcv_a[side, 32:64, :] for side in range(4)]
    w_out = [depth * r_out[side] for side in range(4)]
    w_in = [depth * layer(r_ref, side) for side in range(4)]
    sub32 = iota((32, 128), 0)
    ends = jnp.where((sub32 == 0) | (sub32 == 31), 2.0, 1.0)
    flux = jnp.sum(sum_s, axis=0, keepdims=True) + edge_sum
    deltas = []
    for side in range(4):
        delta = w_in[side] * rcv_a[side, 0:32, :]
        deltas.append(delta)
        term = (layer(s_ref, side) + ends) * delta - w_out[side] * layer(v0_ref, side, PAD)
        flux = flux + jnp.sum(term, axis=0, keepdims=True) - rcv_a[side, 64:65, :]
    for corner, (a, b) in enumerate(CORNERS):
        at_a, at_b = 31 * (b - 2), 31 * a
        flux = flux - (w_out[a][at_a : at_a + 1] + w_out[b][at_b : at_b + 1]) * drcv[0, corner, 0:1, :]
    res = jnp.sum(sum_f, axis=0, keepdims=True) - depth * flux
    own_res = jnp.sum(res, axis=1, keepdims=True)
    row[8:9, :] = jnp.broadcast_to(own_res, (1, 128))
    gather_start(1, gb1)

    for side in range(4):
        add_layer(v1_ref, side, deltas[side], PAD)
    for k in range(ROWS // CHUNK):
        v0_ref[PAD + k * CHUNK : PAD + (k + 1) * CHUNK, :] = sweep(v1_ref, k * CHUNK, CHUNK)
    for side in range(4):
        snd_b[side, 0:32, :] = layer(v1_ref, side, PAD)
        snd_b[side, 32:64, :] = layer(v0_ref, side, PAD)
    sent_b = exchange(snd_b, rcv_b, 4, v1_ref)

    arrive(sent_b)
    outside = []
    for side in range(4):
        add_layer(v0_ref, side, w_in[side] * rcv_b[side, 0:32, :], PAD)
        outside.append(rcv_b[side, 32:64, :] + w_out[side] * layer(v1_ref, side, PAD))
    along = ((0, 1), (2, 3), (0, 2), (1, 3))
    for side in range(4):
        first, last = (drcv[1, corner, 0:1, :] for corner in along[side])
        tip = jnp.where(sub32 == 0, first, jnp.where(sub32 == 31, last, 0.0))
        outside[side] = outside[side] + w_out[side] * tip

    level = 4.0 * depth + up + down
    for k in range(ROWS // CHUNK):
        lo = k * CHUNK
        base_ref[lo : lo + CHUNK, :] = sweep(v0_ref, lo, CHUNK)
    for side in range(4):
        add_layer(base_ref, side, w_in[side] * outside[side])
    for k in range(ROWS // CHUNK):
        lo = k * CHUNK
        v1_ref[PAD + lo : PAD + lo + CHUNK, :] = 0.2 + r_ref[lo : lo + CHUNK, :] * level
    for k in range(ROWS // CHUNK):
        lo = k * CHUNK
        unit_ref[lo : lo + CHUNK, :] = sweep(v1_ref, lo, CHUNK, forced=False)
    w_next = [
        depth * r_ref[32:64, :],
        depth * r_ref[ROWS - 64 : ROWS - 32, :],
        depth * r_ref[pl.ds(1, 32, stride=32), :],
        depth * r_ref[pl.ds(30, 32, stride=32), :],
    ]

    gather_above()
    gather_middle(0, ga1, ga2)
    gather_middle(1, gb1, gb2)
    gather_end(0, ga2)
    columns = coarse_factor(ga2, w0, n0)

    gather_end(1, gb2)
    total = jnp.zeros((8, 128), f32)
    for c in range(4):
        for p in range(2):
            total = total + columns[c, p] * gb2[pl.ds(8 * p + c, 8, stride=16), :]
    line = jnp.sum(total, axis=0, keepdims=True)
    line = jnp.where(iota((8, 128), 1) % 8 == iota((8, 128), 0), line, 0.0)
    near = jnp.sum(line, axis=1, keepdims=True) / ztotal
    near = jnp.broadcast_to(near, (8, 128))
    e = [near[k : k + 1, :] for k in range(8)]
    e0 = (own_res / ztotal + 32.0 * (e[0] + e[1] + e[2] + e[3])) / (128.0 + own_drag)
    edge, inner = [], []
    for side in range(4):
        first, last = (e[4 + corner] - e[side] for corner in along[side])
        jump = jnp.where(sub32 == 0, first, jnp.where(sub32 == 31, last, 0.0))
        beyond = (0.2 + r_out[side] * level) * e[side] + w_out[side] * ((e0 - e[side]) + jump)
        d = w_in[side] * (e[side] - e0)
        near = jnp.where(sub32 == 0, 0.0, pltpu.roll(d, 1, 0)) + jnp.where(sub32 == 31, 0.0, pltpu.roll(d, 31, 0))
        vert = up * pltpu.roll(d, 127, 1) + down * pltpu.roll(d, 1, 1)
        edge.append(0.2 * d + w_in[side] * (near + beyond) + layer(r_ref, side) * vert)
        inner.append(w_next[side] * d)
    stores = []
    ni = CHUNK // 32
    for k in range(ROWS // CHUNK):
        lo = k * CHUNK
        base_ref[lo : lo + CHUNK, :] = base_ref[lo : lo + CHUNK, :] + e0 * unit_ref[lo : lo + CHUNK, :]
        if k == 0:
            base_ref[0:32, :] = base_ref[0:32, :] + edge[0]
            base_ref[32:64, :] = base_ref[32:64, :] + inner[0]
        if k == ROWS // CHUNK - 1:
            base_ref[ROWS - 32 : ROWS, :] = base_ref[ROWS - 32 : ROWS, :] + edge[1]
            base_ref[ROWS - 64 : ROWS - 32, :] = base_ref[ROWS - 64 : ROWS - 32, :] + inner[1]
        for at, part in ((0, edge[2]), (1, inner[2]), (31, edge[3]), (30, inner[3])):
            cells = pl.ds(lo + at, ni, stride=32)
            base_ref[cells, :] = base_ref[cells, :] + part[k * ni : (k + 1) * ni]
        stores.append(
            pltpu.make_async_copy(base_ref.at[pl.ds(lo, CHUNK)], out_hbm.at[pl.ds(lo, CHUNK)], store.at[k])
        )
        stores[-1].start()

    for c in stores:
        c.wait()
    for there, copy, _ in sent_a + sent_b:
        pl.when(there)(copy.wait_send)
    gather_close(0, ga1, ga2)
    gather_close(1, gb1, gb2)


def local(forcing, classes, drag, depth):
    hbm = pl.BlockSpec(memory_space=pltpu.HBM)
    field = pltpu.VMEM((ROWS, 128), f32)
    padded = pltpu.VMEM((ROWS + 2 * PAD, 128), f32)
    out = pl.pallas_call(
        kernel,
        out_shape=jax.ShapeDtypeStruct((ROWS, 128), f32),
        in_specs=[hbm] * 4,
        out_specs=hbm,
        scratch_shapes=[
            field, pltpu.VMEM((32, 32), jnp.int32), pltpu.SMEM((4,), f32), pltpu.VMEM((1, 128), f32),
            field, field, padded, padded, field, field,
            pltpu.VMEM((16, 128), f32),
            pltpu.VMEM((NN, 128), f32), pltpu.VMEM((8 * NW, 128), f32),
            pltpu.VMEM((NN, 128), f32), pltpu.VMEM((8 * NW, 128), f32),
            pltpu.VMEM((4, 72, 128), f32), pltpu.VMEM((4, 72, 128), f32),
            pltpu.VMEM((4, 64, 128), f32), pltpu.VMEM((4, 64, 128), f32),
            pltpu.VMEM((2, 4, 8, 128), f32), pltpu.VMEM((2, 4, 8, 128), f32),
            pltpu.SemaphoreType.DMA((4,)), pltpu.SemaphoreType.DMA((4,)), pltpu.SemaphoreType.DMA((4,)),
            pltpu.SemaphoreType.DMA((8,)), pltpu.SemaphoreType.DMA((8,)),
            pltpu.SemaphoreType.DMA((8,)), pltpu.SemaphoreType.DMA((8,)), pltpu.SemaphoreType.REGULAR,
            pltpu.SemaphoreType.DMA((ROWS // CHUNK,)),
        ],
        compiler_params=pltpu.CompilerParams(
            collective_id=0, has_side_effects=True, vmem_limit_bytes=58 * 1024 * 1024
        ),
        name="vcycle",
    )(forcing.reshape(ROWS, 128), classes, drag, depth.reshape(1, 128))
    return out.reshape(forcing.shape)


def solution(mesh):
    in_specs = (P("wide", "narrow", None), P("wide", "narrow"), P(), P())
    out_specs = P("wide", "narrow", None)
    return jax.shard_map(local, mesh=mesh, in_specs=in_specs, out_specs=out_specs, check_vma=False)
```

time: 53.2 us -> 43.8 us (0.82)
  Pallas kernels: 49.7 us -> 41.8 us
  local copies, waits for them, and re-layouts: 3.22 us -> 1.87 us
    pallas_call x1, Pallas kernels: 49.7 us -> 41.8 us  [local(): pl.pallas_call(kernel, out_shape=jax.ShapeDtypeStruct((ROWS, 128), f32),...]
    unnamed x9 -> x1, local copies, waits for them, and re-layouts: 3.22 us -> 1.87 us
where the time goes in v2:
time: 43.8 us; the launch traced here: 43.6 us
  Pallas kernels  41.8 us (95%)
  local copies, waits for them, and re-layouts  1.87 us (4%)
    pallas_call x1, Pallas kernels, local(): pl.pallas_call(kernel, out_shape=jax.ShapeDtypeStruct((ROWS, 128), f32),...  41.8 us
    unnamed x1, local copies, waits for them, and re-layouts  1.87 us

profile of v2, /device:TPU:1, one launch (start us, length us, event | category | flops | bytes accessed | tf_op | source)
XLA Modules:
  0.0 43.6 jit_solution(18390248089954401138)
XLA Ops:
  0.0 41.8 %vcycle.1 = f32[1024,128]{1,0:T(8,128)} custom-call(f32[1024,128]{1,0:T(8,128)} %bitcast.4, s32[32,32]{1,0:T(8,128)} %cls_hbm.1, f32[4]{0:T(128)} %drag_hbm.1, f32[1,128]{1,0:T(1,128)} %bitcast.5), custom_call_target="tpu_custom_call" | custom-call | tf_op jit(solution)/shard_map/vcycle/pallas_call | solution.py:503
  41.8 1.9 %copy.6 = f32[32,32,128]{2,1,0:T(8,128)} copy(f32[32,32,128]{2,1,0:T(8,128)} %bitcast.3) | data formatting | bytes 1048576

commit v3 on v2

--- a/solution.py
+++ b/solution.py
@@ -141,11 +141,11 @@
 
 
 def kernel(
-    f_hbm, cls_hbm, drag_hbm, depth_hbm, out_hbm,
+    f_hbm, cls_hbm, drag_hbm, depth_hbm, out_ref,
     f_ref, cls_ref, drag_ref, depth_ref,
     r_ref, s_ref, v0_ref, v1_ref, base_ref, unit_ref,
     row, ga1, ga2, gb1, gb2, snd_a, rcv_a, snd_b, rcv_b, dsnd, drcv,
-    load, gs, gr, hs, hr, ds, dr, credit, store,
+    load, gs, gr, hs, hr, ds, dr, credit, ring,
 ):
     w0, n0 = lax.axis_index("wide"), lax.axis_index("narrow")
     z0, x0 = n0 // 4, n0 % 4
@@ -172,9 +172,12 @@
     diags = tuple((sides[a][0], sides[b][1]) for a, b in CORNERS)
     dexist = tuple(exist[a] & exist[b] for a, b in CORNERS)
 
-    def greet_wide(p, _):
-        greet((w0 + p) % NW, n0)
-        return 0
+    y0, c0 = w0 // 2, w0 % 2
+    ring_next = (((y0 + 1) % 8) * 2 + c0, ((y0 + 7) % 8) * 2 + c0)
+
+    def relay(k):
+        for w in ring_next:
+            pl.semaphore_signal(ring.at[k], inc=1, device_id=(w, n0), device_id_type=MESH)
 
     def greet_above(n, _):
         greet(w0, n)
@@ -185,7 +188,10 @@
     for t, there in zip(diags, dexist):
         pl.when(there)(functools.partial(greet, *t))
     pl.when((x0 == 0) & (z0 > 0))(functools.partial(greet, w0, n0 - 1))
-    lax.fori_loop(1, NW, greet_wide, 0)
+    greet(y0 * 2 + (1 - c0), n0)
+    for dy in (1, 7):
+        for c in (0, 1):
+            greet(((y0 + dy) % 8) * 2 + c, n0)
     lax.fori_loop(4 * z0 + 4, NN, greet_above, 0)
 
     for side in range(4):
@@ -272,15 +278,15 @@
             slot = base // 4
             dsnd[slot, corner, 0:1, :] = corner_src[PAD + CORNER_ROW[corner] : PAD + CORNER_ROW[corner] + 1, :]
             copy = pltpu.make_async_remote_copy(
-                src_ref=dsnd.at[slot, corner], dst_ref=drcv.at[slot, 3 - corner], send_sem=ds.at[base + corner],
+                src_ref=dsnd.at[slot, corner, pl.ds(0, 1)], dst_ref=drcv.at[slot, 3 - corner, pl.ds(0, 1)], send_sem=ds.at[base + corner],
                 recv_sem=dr.at[base + 3 - corner], device_id=t, device_id_type=MESH,
             )
             mirror = pltpu.make_async_remote_copy(
-                src_ref=dsnd.at[slot, corner], dst_ref=drcv.at[slot, corner], send_sem=ds.at[base + corner],
+                src_ref=dsnd.at[slot, corner, pl.ds(0, 1)], dst_ref=drcv.at[slot, corner, pl.ds(0, 1)], send_sem=ds.at[base + corner],
                 recv_sem=dr.at[base + corner], device_id=t, device_id_type=MESH,
             )
             copies.append((dexist[corner], copy, mirror))
-        for there, copy, _ in copies:
+        for there, copy, _ in copies[4:] + copies[:4]:
             pl.when(there)(copy.start)
         return copies
 
@@ -297,10 +303,11 @@
         edge_sum = edge_sum + total
         snd_a[side, 64:72, :] = jnp.broadcast_to(total, (8, 128))
 
-    hello = 4 * z0 + 3 + (NW - 1) + jnp.where((x0 == 3) & (z0 < 15), 1, 0)
+    hello = 4 * z0 + 3 + 5 + jnp.where((x0 == 3) & (z0 < 15), 1, 0)
     for there in dexist:
         hello = hello + jnp.where(there, 1, 0)
     pl.semaphore_wait(bar, hello)
+    relay(0)
 
     sub16, lane16 = iota((16, 128), 0), iota((16, 128), 1)
     mine = x0 * 16 + z0
@@ -345,11 +352,11 @@
             jnp.sum(jnp.where(lane16 // 8 == sub16, buf[16 * x : 16 * x + 16, :], 0.0), axis=0, keepdims=True)
             for x in range(4)
         ]
-        buf2[pl.ds(at, 8), :] = jnp.concatenate(rows + rows, axis=0)
+        buf2[pl.ds(at, 4), :] = jnp.concatenate(rows, axis=0)
 
         def send(p, _):
             pltpu.make_async_remote_copy(
-                src_ref=buf2.at[pl.ds(at, 8)], dst_ref=buf2.at[pl.ds(at, 8)], send_sem=gs.at[2 * k + 1],
+                src_ref=buf2.at[pl.ds(at, 4)], dst_ref=buf2.at[pl.ds(at, 4)], send_sem=gs.at[2 * k + 1],
                 recv_sem=gr.at[2 * k + 1], device_id=((w0 + p) % NW, n0), device_id_type=MESH,
             ).start()
             return 0
@@ -357,11 +364,11 @@
         lax.fori_loop(1, NW, send, 0)
 
     def gather_end(k, buf2):
-        drain(buf2, 8 * (NW - 1), gr.at[2 * k + 1])
+        drain(buf2, 4 * (NW - 1), gr.at[2 * k + 1])
 
     def gather_close(k, buf, buf2):
         drain(buf, NN - 1, gs.at[2 * k])
-        drain(buf2, 8 * (NW - 1), gs.at[2 * k + 1])
+        drain(buf2, 4 * (NW - 1), gs.at[2 * k + 1])
 
     sent_a = exchange(snd_a, rcv_a, 0, v0_ref)
     s2d = jnp.where(kinds == 0, drags[0], jnp.where(kinds == 1, drags[1], jnp.where(kinds == 2, drags[2], drags[3])))
@@ -382,7 +389,11 @@
         v1_ref[PAD + lo : PAD + lo + CHUNK, :] = v
         sum_s = sum_s + jnp.sum((s_ref[lo : lo + CHUNK, :] * v).reshape(CHUNK // 8, 8, 128), axis=0)
 
+    pl.semaphore_wait(ring.at[0], 2)
+    relay(1)
     arrive(sent_a)
+    pl.semaphore_wait(ring.at[1], 2)
+    relay(2)
     r_out = [rcv_a[side, 32:64, :] for side in range(4)]
     w_out = [depth * r_out[side] for side in range(4)]
     w_in = [depth * layer(r_ref, side) for side in range(4)]
@@ -443,6 +454,7 @@
     ]
 
     gather_above()
+    pl.semaphore_wait(ring.at[2], 2)
     gather_middle(0, ga1, ga2)
     gather_middle(1, gb1, gb2)
     gather_end(0, ga2)
@@ -469,27 +481,16 @@
         vert = up * pltpu.roll(d, 127, 1) + down * pltpu.roll(d, 1, 1)
         edge.append(0.2 * d + w_in[side] * (near + beyond) + layer(r_ref, side) * vert)
         inner.append(w_next[side] * d)
-    stores = []
-    ni = CHUNK // 32
     for k in range(ROWS // CHUNK):
         lo = k * CHUNK
-        base_ref[lo : lo + CHUNK, :] = base_ref[lo : lo + CHUNK, :] + e0 * unit_ref[lo : lo + CHUNK, :]
-        if k == 0:
-            base_ref[0:32, :] = base_ref[0:32, :] + edge[0]
-            base_ref[32:64, :] = base_ref[32:64, :] + inner[0]
-        if k == ROWS // CHUNK - 1:
-            base_ref[ROWS - 32 : ROWS, :] = base_ref[ROWS - 32 : ROWS, :] + edge[1]
-            base_ref[ROWS - 64 : ROWS - 32, :] = base_ref[ROWS - 64 : ROWS - 32, :] + inner[1]
-        for at, part in ((0, edge[2]), (1, inner[2]), (31, edge[3]), (30, inner[3])):
-            cells = pl.ds(lo + at, ni, stride=32)
-            base_ref[cells, :] = base_ref[cells, :] + part[k * ni : (k + 1) * ni]
-        stores.append(
-            pltpu.make_async_copy(base_ref.at[pl.ds(lo, CHUNK)], out_hbm.at[pl.ds(lo, CHUNK)], store.at[k])
-        )
-        stores[-1].start()
-
-    for c in stores:
-        c.wait()
+        out_ref[lo : lo + CHUNK, :] = base_ref[lo : lo + CHUNK, :] + e0 * unit_ref[lo : lo + CHUNK, :]
+    out_ref[32:64, :] = out_ref[32:64, :] + inner[0]
+    out_ref[ROWS - 64 : ROWS - 32, :] = out_ref[ROWS - 64 : ROWS - 32, :] + inner[1]
+    for at, part in ((1, inner[2]), (30, inner[3])):
+        out_ref[pl.ds(at, 32, stride=32), :] = out_ref[pl.ds(at, 32, stride=32), :] + part
+    for side in range(4):
+        add_layer(out_ref, side, edge[side])
+
     for there, copy, _ in sent_a + sent_b:
         pl.when(there)(copy.wait_send)
     gather_close(0, ga1, ga2)
@@ -500,11 +501,12 @@
     hbm = pl.BlockSpec(memory_space=pltpu.HBM)
     field = pltpu.VMEM((ROWS, 128), f32)
     padded = pltpu.VMEM((ROWS + 2 * PAD, 128), f32)
+    args = (forcing.reshape(ROWS, 128), classes, drag, depth.reshape(1, 128))
     out = pl.pallas_call(
         kernel,
-        out_shape=jax.ShapeDtypeStruct((ROWS, 128), f32),
+        out_shape=pltpu.VMEM((ROWS, 128), f32),
         in_specs=[hbm] * 4,
-        out_specs=hbm,
+        out_specs=pl.BlockSpec(memory_space=pltpu.VMEM),
         scratch_shapes=[
             field, pltpu.VMEM((32, 32), jnp.int32), pltpu.SMEM((4,), f32), pltpu.VMEM((1, 128), f32),
             field, field, padded, padded, field, field,
@@ -517,13 +519,13 @@
             pltpu.SemaphoreType.DMA((4,)), pltpu.SemaphoreType.DMA((4,)), pltpu.SemaphoreType.DMA((4,)),
             pltpu.SemaphoreType.DMA((8,)), pltpu.SemaphoreType.DMA((8,)),
             pltpu.SemaphoreType.DMA((8,)), pltpu.SemaphoreType.DMA((8,)), pltpu.SemaphoreType.REGULAR,
-            pltpu.SemaphoreType.DMA((ROWS // CHUNK,)),
+            pltpu.SemaphoreType.REGULAR((3,)),
         ],
         compiler_params=pltpu.CompilerParams(
-            collective_id=0, has_side_effects=True, vmem_limit_bytes=58 * 1024 * 1024
+            collective_id=0, has_side_effects=True, vmem_limit_bytes=40 * 1024 * 1024
         ),
         name="vcycle",
-    )(forcing.reshape(ROWS, 128), classes, drag, depth.reshape(1, 128))
+    )(*(pltpu.with_memory_space_constraint(a, pltpu.HBM) for a in args))
     return out.reshape(forcing.shape)
 
 

time: 43.8 us -> 41.1 us (0.938)
  Pallas kernels: 41.8 us -> 40.1 us
  local copies, waits for them, and re-layouts: 1.87 us -> 0.8 us
    pallas_call x1, Pallas kernels: 41.8 us -> 40.1 us  [local(): pl.pallas_call(kernel, out_shape=pltpu.VMEM((ROWS, 128), f32), in_specs=[...]
    unnamed x1, local copies, waits for them, and re-layouts: 1.87 us -> 0.8 us
where the time goes in v3:
time: 41.1 us; the launch traced here: 40.9 us
  Pallas kernels  40.1 us (98%)
  local copies, waits for them, and re-layouts  0.8 us (2%)
    pallas_call x1, Pallas kernels, local(): pl.pallas_call(kernel, out_shape=pltpu.VMEM((ROWS, 128), f32), in_specs=[...  40.1 us

profile of v3, /device:TPU:1, one launch (start us, length us, event | category | flops | bytes accessed | tf_op | source)
XLA Modules:
  0.0 40.9 jit_solution(15455949941601129873)
XLA Ops:
  0.0 40.1 %vcycle.1 = f32[1024,128]{1,0:T(8,128)S(1)} custom-call(f32[1024,128]{1,0:T(8,128)} %bitcast.4, s32[32,32]{1,0:T(8,128)} %cls_hbm.1, f32[4]{0:T(128)} %drag_hbm.1, f32[1,128]{1,0:T(1,128)} %bitcast.5), custom_call_target="tpu_custom_call" | custom-call | tf_op jit(solution)/shard_map/vcycle/pallas_call | solution.py:505
  40.1 0.8 %copy.6 = f32[32,32,128]{2,1,0:T(8,128)} copy(f32[32,32,128]{2,1,0:T(8,128)S(1)} %bitcast.3) | data formatting | bytes 1048576

commit v4 on v3

--- a/solution.py
+++ b/solution.py
@@ -137,13 +137,23 @@
         out[c, color(c, 0)] = x[c, color(c, 0)]
         p = color(c, 1)
         out[c, p] = b[c, p] + q[c, p] * gather(x, c, p)
-    return out
+
+    parts = {}
+    for c in range(4):
+        for p in range(2):
+            flip = out[c, 1 - p]
+            low = jnp.where(sub == 0, 0.0, pltpu.roll(flip, 1, 0)) if p == 0 else flip
+            high = flip if p == 0 else jnp.where(sub == 7, 0.0, pltpu.roll(flip, 7, 0))
+            left = out[c - 1, p] if c > 0 else shifted(out[3, p], -1)
+            right = out[c + 1, p] if c < 3 else shifted(out[0, p], 1)
+            parts[c, p] = [out[c, p]] + [beyond - out[c, p] for beyond in (low, high, left, right)]
+    return parts
 
 
 def kernel(
     f_hbm, cls_hbm, drag_hbm, depth_hbm, out_ref,
     f_ref, cls_ref, drag_ref, depth_ref,
-    r_ref, s_ref, v0_ref, v1_ref, base_ref, unit_ref,
+    r_ref, s_ref, v0_ref, v1_ref, base_ref, unit_ref, pick_ref,
     row, ga1, ga2, gb1, gb2, snd_a, rcv_a, snd_b, rcv_b, dsnd, drcv,
     load, gs, gr, hs, hr, ds, dr, credit, ring,
 ):
@@ -185,8 +195,6 @@
 
     for p in range(1, 4):
         greet(w0, beside_x(p))
-    for t, there in zip(diags, dexist):
-        pl.when(there)(functools.partial(greet, *t))
     pl.when((x0 == 0) & (z0 > 0))(functools.partial(greet, w0, n0 - 1))
     greet(y0 * 2 + (1 - c0), n0)
     for dy in (1, 7):
@@ -198,15 +206,14 @@
 
         @pl.when(jnp.logical_not(exist[side]))
         def _(side=side):
-            rcv_a[side] = jnp.zeros((72, 128), f32)
-            rcv_b[side] = jnp.zeros((64, 128), f32)
+            rcv_a[side] = jnp.zeros((32, 128), f32)
+            rcv_b[side] = jnp.zeros((96, 128), f32)
 
     for corner in range(4):
 
         @pl.when(jnp.logical_not(dexist[corner]))
         def _(corner=corner):
-            drcv[0, corner] = jnp.zeros((8, 128), f32)
-            drcv[1, corner] = jnp.zeros((8, 128), f32)
+            drcv[corner] = jnp.zeros((8, 128), f32)
 
     zpad = jnp.zeros((PAD, 128), f32)
     for ref in (v0_ref, v1_ref):
@@ -225,6 +232,117 @@
 
     kinds = cls_ref[...]
 
+    def sweep(src, lo, n, forced=True):
+        jpos = iota((n, 128), 0) % 32
+        c = src[PAD + lo : PAD + lo + n, :]
+        near = src[lo : lo + n, :] + src[2 * PAD + lo : 2 * PAD + lo + n, :]
+        near = near + jnp.where(jpos == 0, 0.0, src[PAD + lo - 1 : PAD + lo - 1 + n, :])
+        near = near + jnp.where(jpos == 31, 0.0, src[PAD + lo + 1 : PAD + lo + 1 + n, :])
+        force = depth * near + (up * pltpu.roll(c, 127, 1) + down * pltpu.roll(c, 1, 1))
+        if forced:
+            force = f_ref[lo : lo + n, :] + force
+        return 0.2 * c + r_ref[lo : lo + n, :] * force
+
+    def exchange(snd, rcv, base, corners):
+        copies = []
+        for side, t in enumerate(sides):
+            copy = pltpu.make_async_remote_copy(
+                src_ref=snd.at[side], dst_ref=rcv.at[side ^ 1], send_sem=hs.at[base + side],
+                recv_sem=hr.at[base + (side ^ 1)], device_id=t, device_id_type=MESH,
+            )
+            mirror = pltpu.make_async_remote_copy(
+                src_ref=snd.at[side], dst_ref=rcv.at[side], send_sem=hs.at[base + side],
+                recv_sem=hr.at[base + side], device_id=t, device_id_type=MESH,
+            )
+            copies.append((exist[side], copy, mirror))
+        for corner, t in enumerate(diags if corners else ()):
+            copy = pltpu.make_async_remote_copy(
+                src_ref=dsnd.at[corner, pl.ds(0, 1)], dst_ref=drcv.at[3 - corner, pl.ds(0, 1)],
+                send_sem=ds.at[corner], recv_sem=dr.at[3 - corner], device_id=t, device_id_type=MESH,
+            )
+            mirror = pltpu.make_async_remote_copy(
+                src_ref=dsnd.at[corner, pl.ds(0, 1)], dst_ref=drcv.at[corner, pl.ds(0, 1)],
+                send_sem=ds.at[corner], recv_sem=dr.at[corner], device_id=t, device_id_type=MESH,
+            )
+            copies.append((dexist[corner], copy, mirror))
+        for there, copy, _ in copies:
+            pl.when(there)(copy.start)
+        return copies
+
+    def arrive(copies):
+        for there, _, mirror in copies:
+            pl.when(there)(mirror.wait_recv)
+
+    s2d = jnp.where(kinds == 0, drags[0], jnp.where(kinds == 1, drags[1], jnp.where(kinds == 2, drags[2], drags[3])))
+    own_drag = jnp.sum(jnp.sum(s2d, axis=0, keepdims=True), axis=1, keepdims=True) * (1.0 / ROWS)
+    row[0:1, :] = jnp.broadcast_to(own_drag, (1, 128))
+    hello = 4 * z0 + 3 + 5 + jnp.where((x0 == 3) & (z0 < 15), 1, 0)
+    pl.semaphore_wait(bar, hello)
+    relay(0)
+
+    sub16, lane16 = iota((16, 128), 0), iota((16, 128), 1)
+    mine = x0 * 16 + z0
+
+    def drain(buf, rows, sem):
+        pltpu.make_async_copy(buf.at[pl.ds(0, rows)], buf.at[pl.ds(0, rows)], sem).wait()
+
+    def narrow_send(k, buf, n):
+        pltpu.make_async_remote_copy(
+            src_ref=row.at[pl.ds(8 * k, 1)], dst_ref=buf.at[pl.ds(mine, 1)], send_sem=gs.at[2 * k],
+            recv_sem=gr.at[2 * k], device_id=(w0, n), device_id_type=MESH,
+        ).start()
+
+    def gather_start(k, buf, lo, hi, last=True):
+        def send(n, _):
+            narrow_send(k, buf, n)
+            return 0
+
+        lax.fori_loop(lo, hi, send, 0)
+        if last:
+            buf[pl.ds(mine, 1), :] = row[8 * k : 8 * k + 1, :]
+            for p in range(1, 4):
+                narrow_send(k, buf, beside_x(p))
+
+    def gather_above():
+        @pl.when(z0 < 15)
+        def _():
+            pl.semaphore_wait(credit, 4 * (15 - z0))
+
+
+        def send(n, _):
+            narrow_send(0, ga1, n)
+            narrow_send(1, gb1, n)
+            return 0
+
+        lax.fori_loop(4 * z0 + 4, NN, send, 0)
+
+    def gather_middle(k, buf, buf2):
+        drain(buf, NN - 1, gr.at[2 * k])
+        at = pl.multiple_of(w0 * 8, 8)
+        rows = [
+            jnp.sum(jnp.where(lane16 // 8 == sub16, buf[16 * x : 16 * x + 16, :], 0.0), axis=0, keepdims=True)
+            for x in range(4)
+        ]
+        buf2[pl.ds(at, 4), :] = jnp.concatenate(rows, axis=0)
+
+        def send(p, _):
+            pltpu.make_async_remote_copy(
+                src_ref=buf2.at[pl.ds(at, 4)], dst_ref=buf2.at[pl.ds(at, 4)], send_sem=gs.at[2 * k + 1],
+                recv_sem=gr.at[2 * k + 1], device_id=((w0 + p) % NW, n0), device_id_type=MESH,
+            ).start()
+            return 0
+
+        lax.fori_loop(1, NW, send, 0)
+
+    def gather_end(k, buf2):
+        drain(buf2, 4 * (NW - 1), gr.at[2 * k + 1])
+
+    def gather_close(k, buf, buf2):
+        drain(buf, NN - 1, gs.at[2 * k])
+        drain(buf2, 4 * (NW - 1), gs.at[2 * k + 1])
+
+    urgent = jnp.minimum(4 * z0, 16)
+    gather_start(0, ga1, 0, urgent, last=False)
     cf = kinds.astype(f32)
     eye = jnp.where(iota((32, 32), 0) == iota((32, 32), 1), 1.0, 0.0).astype(f32)
     ones = jnp.ones((32, 128), f32)
@@ -243,138 +361,10 @@
         v0_ref[PAD + k * CHUNK : PAD + (k + 1) * CHUNK, :] = rr * f
         sum_f = sum_f + jnp.sum(f.reshape(CHUNK // 8, 8, 128), axis=0)
 
-    def sweep(src, lo, n, forced=True):
-        jpos = iota((n, 128), 0) % 32
-        c = src[PAD + lo : PAD + lo + n, :]
-        near = src[lo : lo + n, :] + src[2 * PAD + lo : 2 * PAD + lo + n, :]
-        near = near + jnp.where(jpos == 0, 0.0, src[PAD + lo - 1 : PAD + lo - 1 + n, :])
-        near = near + jnp.where(jpos == 31, 0.0, src[PAD + lo + 1 : PAD + lo + 1 + n, :])
-        force = depth * near + (up * pltpu.roll(c, 127, 1) + down * pltpu.roll(c, 1, 1))
-        if forced:
-            force = f_ref[lo : lo + n, :] + force
-        return 0.2 * c + r_ref[lo : lo + n, :] * force
-
-    def sweep_column(src, side):
-        at = 0 if side == 2 else 31
-        c = src[pl.ds(PAD + at, 32, stride=32), :]
-        near = src[pl.ds(at, 32, stride=32), :] + src[pl.ds(2 * PAD + at, 32, stride=32), :]
-        near = near + src[pl.ds(PAD + (1 if side == 2 else 30), 32, stride=32), :]
-        force = depth * near + (up * pltpu.roll(c, 127, 1) + down * pltpu.roll(c, 1, 1))
-        return 0.2 * c + layer(r_ref, side) * (layer(f_ref, side) + force)
-
-    def exchange(snd, rcv, base, corner_src):
-        copies = []
-        for side, t in enumerate(sides):
-            copy = pltpu.make_async_remote_copy(
-                src_ref=snd.at[side], dst_ref=rcv.at[side ^ 1], send_sem=hs.at[base + side],
-                recv_sem=hr.at[base + (side ^ 1)], device_id=t, device_id_type=MESH,
-            )
-            mirror = pltpu.make_async_remote_copy(
-                src_ref=snd.at[side], dst_ref=rcv.at[side], send_sem=hs.at[base + side],
-                recv_sem=hr.at[base + side], device_id=t, device_id_type=MESH,
-            )
-            copies.append((exist[side], copy, mirror))
-        for corner, t in enumerate(diags):
-            slot = base // 4
-            dsnd[slot, corner, 0:1, :] = corner_src[PAD + CORNER_ROW[corner] : PAD + CORNER_ROW[corner] + 1, :]
-            copy = pltpu.make_async_remote_copy(
-                src_ref=dsnd.at[slot, corner, pl.ds(0, 1)], dst_ref=drcv.at[slot, 3 - corner, pl.ds(0, 1)], send_sem=ds.at[base + corner],
-                recv_sem=dr.at[base + 3 - corner], device_id=t, device_id_type=MESH,
-            )
-            mirror = pltpu.make_async_remote_copy(
-                src_ref=dsnd.at[slot, corner, pl.ds(0, 1)], dst_ref=drcv.at[slot, corner, pl.ds(0, 1)], send_sem=ds.at[base + corner],
-                recv_sem=dr.at[base + corner], device_id=t, device_id_type=MESH,
-            )
-            copies.append((dexist[corner], copy, mirror))
-        for there, copy, _ in copies[4:] + copies[:4]:
-            pl.when(there)(copy.start)
-        return copies
-
-    def arrive(copies):
-        for there, _, mirror in copies:
-            pl.when(there)(mirror.wait_recv)
-
-    edge_sum = jnp.zeros((1, 128), f32)
-    for side in range(4):
-        snd_a[side, 0:32, :] = layer(v0_ref, side, PAD)
-        snd_a[side, 32:64, :] = layer(r_ref, side)
-        swept = sweep(v0_ref, (0, ROWS - 32)[side], 32) if side < 2 else sweep_column(v0_ref, side)
-        total = jnp.sum(swept, axis=0, keepdims=True)
-        edge_sum = edge_sum + total
-        snd_a[side, 64:72, :] = jnp.broadcast_to(total, (8, 128))
-
-    hello = 4 * z0 + 3 + 5 + jnp.where((x0 == 3) & (z0 < 15), 1, 0)
-    for there in dexist:
-        hello = hello + jnp.where(there, 1, 0)
-    pl.semaphore_wait(bar, hello)
-    relay(0)
-
-    sub16, lane16 = iota((16, 128), 0), iota((16, 128), 1)
-    mine = x0 * 16 + z0
-
-    def drain(buf, rows, sem):
-        pltpu.make_async_copy(buf.at[pl.ds(0, rows)], buf.at[pl.ds(0, rows)], sem).wait()
-
-    def narrow_send(k, buf, n):
-        pltpu.make_async_remote_copy(
-            src_ref=row.at[pl.ds(8 * k, 1)], dst_ref=buf.at[pl.ds(mine, 1)], send_sem=gs.at[2 * k],
-            recv_sem=gr.at[2 * k], device_id=(w0, n), device_id_type=MESH,
-        ).start()
-
-    def gather_start(k, buf):
-        buf[pl.ds(mine, 1), :] = row[8 * k : 8 * k + 1, :]
-
-        def send(n, _):
-            narrow_send(k, buf, n)
-            return 0
-
-        lax.fori_loop(0, 4 * z0, send, 0)
-        for p in range(1, 4):
-            narrow_send(k, buf, beside_x(p))
-
-    def gather_above():
-        @pl.when(z0 < 15)
-        def _():
-            pl.semaphore_wait(credit, 4 * (15 - z0))
-
-
-        def send(n, _):
-            narrow_send(0, ga1, n)
-            narrow_send(1, gb1, n)
-            return 0
-
-        lax.fori_loop(4 * z0 + 4, NN, send, 0)
-
-    def gather_middle(k, buf, buf2):
-        drain(buf, NN - 1, gr.at[2 * k])
-        at = pl.multiple_of(w0 * 8, 8)
-        rows = [
-            jnp.sum(jnp.where(lane16 // 8 == sub16, buf[16 * x : 16 * x + 16, :], 0.0), axis=0, keepdims=True)
-            for x in range(4)
-        ]
-        buf2[pl.ds(at, 4), :] = jnp.concatenate(rows, axis=0)
-
-        def send(p, _):
-            pltpu.make_async_remote_copy(
-                src_ref=buf2.at[pl.ds(at, 4)], dst_ref=buf2.at[pl.ds(at, 4)], send_sem=gs.at[2 * k + 1],
-                recv_sem=gr.at[2 * k + 1], device_id=((w0 + p) % NW, n0), device_id_type=MESH,
-            ).start()
-            return 0
-
-        lax.fori_loop(1, NW, send, 0)
-
-    def gather_end(k, buf2):
-        drain(buf2, 4 * (NW - 1), gr.at[2 * k + 1])
-
-    def gather_close(k, buf, buf2):
-        drain(buf, NN - 1, gs.at[2 * k])
-        drain(buf2, 4 * (NW - 1), gs.at[2 * k + 1])
-
-    sent_a = exchange(snd_a, rcv_a, 0, v0_ref)
-    s2d = jnp.where(kinds == 0, drags[0], jnp.where(kinds == 1, drags[1], jnp.where(kinds == 2, drags[2], drags[3])))
-    own_drag = jnp.sum(jnp.sum(s2d, axis=0, keepdims=True), axis=1, keepdims=True) * (1.0 / ROWS)
-    row[0:1, :] = jnp.broadcast_to(own_drag, (1, 128))
-    gather_start(0, ga1)
+    for side in range(4):
+        snd_a[side] = layer(v0_ref, side, PAD)
+    sent_a = exchange(snd_a, rcv_a, 0, False)
+    gather_start(0, ga1, urgent, 4 * z0)
 
     def give_credit(n, _):
         pl.semaphore_signal(credit, inc=1, device_id=(w0, n), device_id_type=MESH)
@@ -394,43 +384,47 @@
     arrive(sent_a)
     pl.semaphore_wait(ring.at[1], 2)
     relay(2)
-    r_out = [rcv_a[side, 32:64, :] for side in range(4)]
-    w_out = [depth * r_out[side] for side in range(4)]
     w_in = [depth * layer(r_ref, side) for side in range(4)]
     sub32 = iota((32, 128), 0)
-    ends = jnp.where((sub32 == 0) | (sub32 == 31), 2.0, 1.0)
-    flux = jnp.sum(sum_s, axis=0, keepdims=True) + edge_sum
-    deltas = []
-    for side in range(4):
-        delta = w_in[side] * rcv_a[side, 0:32, :]
-        deltas.append(delta)
-        term = (layer(s_ref, side) + ends) * delta - w_out[side] * layer(v0_ref, side, PAD)
-        flux = flux + jnp.sum(term, axis=0, keepdims=True) - rcv_a[side, 64:65, :]
-    for corner, (a, b) in enumerate(CORNERS):
-        at_a, at_b = 31 * (b - 2), 31 * a
-        flux = flux - (w_out[a][at_a : at_a + 1] + w_out[b][at_b : at_b + 1]) * drcv[0, corner, 0:1, :]
-    res = jnp.sum(sum_f, axis=0, keepdims=True) - depth * flux
-    own_res = jnp.sum(res, axis=1, keepdims=True)
-    row[8:9, :] = jnp.broadcast_to(own_res, (1, 128))
-    gather_start(1, gb1)
-
-    for side in range(4):
-        add_layer(v1_ref, side, deltas[side], PAD)
+    drained = jnp.sum(sum_s, axis=0, keepdims=True)
+    for side in range(4):
+        delta = w_in[side] * rcv_a[side]
+        drained = drained + jnp.sum(layer(s_ref, side) * delta, axis=0, keepdims=True)
+        add_layer(v1_ref, side, delta, PAD)
+    own_part = jnp.sum(sum_f, axis=0, keepdims=True) - depth * drained
+    leaves = [depth * jnp.sum(layer(v1_ref, side, PAD), axis=0, keepdims=True) for side in range(4)]
+    sub8, lane8 = iota((8, 128), 0), iota((8, 128), 1)
+    stack = jnp.where(sub8 == 0, own_part, 0.0)
+    for side in range(4):
+        stack = jnp.where(sub8 == side + 1, leaves[side], stack)
+    five = jnp.broadcast_to(jnp.sum(stack, axis=1, keepdims=True), (8, 128))
+    row[8:9, :] = jnp.sum(jnp.where(lane8 % 8 == sub8, five, 0.0), axis=0, keepdims=True)
+    gather_start(1, gb1, 0, 4 * z0)
+
     for k in range(ROWS // CHUNK):
         v0_ref[PAD + k * CHUNK : PAD + (k + 1) * CHUNK, :] = sweep(v1_ref, k * CHUNK, CHUNK)
     for side in range(4):
         snd_b[side, 0:32, :] = layer(v1_ref, side, PAD)
         snd_b[side, 32:64, :] = layer(v0_ref, side, PAD)
-    sent_b = exchange(snd_b, rcv_b, 4, v1_ref)
+        snd_b[side, 64:96, :] = layer(r_ref, side)
+    for corner, at in enumerate(CORNER_ROW):
+        dsnd[corner, 0:1, :] = v1_ref[PAD + at : PAD + at + 1, :]
+    sent_b = exchange(snd_b, rcv_b, 4, True)
 
     arrive(sent_b)
+    r_out = [rcv_b[side, 64:96, :] for side in range(4)]
+    w_out = [depth * r_out[side] for side in range(4)]
+    res = own_part
+    for side in range(4):
+        res = res - leaves[side] + depth * jnp.sum(rcv_b[side, 0:32, :], axis=0, keepdims=True)
+    own_res = jnp.sum(res, axis=1, keepdims=True)
     outside = []
     for side in range(4):
         add_layer(v0_ref, side, w_in[side] * rcv_b[side, 0:32, :], PAD)
         outside.append(rcv_b[side, 32:64, :] + w_out[side] * layer(v1_ref, side, PAD))
     along = ((0, 1), (2, 3), (0, 2), (1, 3))
     for side in range(4):
-        first, last = (drcv[1, corner, 0:1, :] for corner in along[side])
+        first, last = (drcv[corner, 0:1, :] for corner in along[side])
         tip = jnp.where(sub32 == 0, first, jnp.where(sub32 == 31, last, 0.0))
         outside[side] = outside[side] + w_out[side] * tip
 
@@ -453,18 +447,26 @@
         depth * r_ref[pl.ds(30, 32, stride=32), :],
     ]
 
+    for k in range(5):
+        source, target = iota((128, 128), 0), iota((128, 128), 1)
+        pick_ref[:, 128 * k : 128 * k + 128] = jnp.where(source == target // 8 * 8 + k, 1.0, 0.0).astype(f32)
+
     gather_above()
     pl.semaphore_wait(ring.at[2], 2)
     gather_middle(0, ga1, ga2)
     gather_middle(1, gb1, gb2)
     gather_end(0, ga2)
-    columns = coarse_factor(ga2, w0, n0)
+    parts = coarse_factor(ga2, w0, n0)
 
     gather_end(1, gb2)
+    gathered = jnp.concatenate([gb2[pl.ds(8 * p + c, 8, stride=16), :] for c in range(4) for p in range(2)], axis=0)
+    wide = jnp.dot(gathered, pick_ref[...], precision=lax.Precision.HIGHEST, preferred_element_type=f32)
     total = jnp.zeros((8, 128), f32)
     for c in range(4):
         for p in range(2):
-            total = total + columns[c, p] * gb2[pl.ds(8 * p + c, 8, stride=16), :]
+            at = 8 * (2 * c + p)
+            for k in range(5):
+                total = total + parts[c, p][k] * wide[at : at + 8, 128 * k : 128 * k + 128]
     line = jnp.sum(total, axis=0, keepdims=True)
     line = jnp.where(iota((8, 128), 1) % 8 == iota((8, 128), 0), line, 0.0)
     near = jnp.sum(line, axis=1, keepdims=True) / ztotal
@@ -509,16 +511,16 @@
         out_specs=pl.BlockSpec(memory_space=pltpu.VMEM),
         scratch_shapes=[
             field, pltpu.VMEM((32, 32), jnp.int32), pltpu.SMEM((4,), f32), pltpu.VMEM((1, 128), f32),
-            field, field, padded, padded, field, field,
+            field, field, padded, padded, field, field, pltpu.VMEM((128, 640), f32),
             pltpu.VMEM((16, 128), f32),
             pltpu.VMEM((NN, 128), f32), pltpu.VMEM((8 * NW, 128), f32),
             pltpu.VMEM((NN, 128), f32), pltpu.VMEM((8 * NW, 128), f32),
-            pltpu.VMEM((4, 72, 128), f32), pltpu.VMEM((4, 72, 128), f32),
-            pltpu.VMEM((4, 64, 128), f32), pltpu.VMEM((4, 64, 128), f32),
-            pltpu.VMEM((2, 4, 8, 128), f32), pltpu.VMEM((2, 4, 8, 128), f32),
+            pltpu.VMEM((4, 32, 128), f32), pltpu.VMEM((4, 32, 128), f32),
+            pltpu.VMEM((4, 96, 128), f32), pltpu.VMEM((4, 96, 128), f32),
+            pltpu.VMEM((4, 8, 128), f32), pltpu.VMEM((4, 8, 128), f32),
             pltpu.SemaphoreType.DMA((4,)), pltpu.SemaphoreType.DMA((4,)), pltpu.SemaphoreType.DMA((4,)),
             pltpu.SemaphoreType.DMA((8,)), pltpu.SemaphoreType.DMA((8,)),
-            pltpu.SemaphoreType.DMA((8,)), pltpu.SemaphoreType.DMA((8,)), pltpu.SemaphoreType.REGULAR,
+            pltpu.SemaphoreType.DMA((4,)), pltpu.SemaphoreType.DMA((4,)), pltpu.SemaphoreType.REGULAR,
             pltpu.SemaphoreType.REGULAR((3,)),
         ],
         compiler_params=pltpu.CompilerParams(

time: 41.1 us -> 41 us (level)
  no operation moved by 1% of the time
where the time goes in v4:
time: 41 us; the launch traced here: 40.8 us
  Pallas kernels  40 us (98%)
  local copies, waits for them, and re-layouts  0.8 us (2%)
    pallas_call x1, Pallas kernels, local(): pl.pallas_call(kernel, out_shape=pltpu.VMEM((ROWS, 128), f32), in_specs=[...  40 us

profile of v4, /device:TPU:1, one launch (start us, length us, event | category | flops | bytes accessed | tf_op | source)
XLA Modules:
  0.0 40.8 jit_solution(2511174132452979907)
XLA Ops:
  0.0 40.0 %vcycle.1 = f32[1024,128]{1,0:T(8,128)S(1)} custom-call(f32[1024,128]{1,0:T(8,128)} %bitcast.4, s32[32,32]{1,0:T(8,128)} %cls_hbm.1, f32[4]{0:T(128)} %drag_hbm.1, f32[1,128]{1,0:T(1,128)} %bitcast.5), custom_call_target="tpu_custom_call" | custom-call | tf_op jit(solution)/shard_map/vcycle/pallas_call | solution.py:507
  40.0 0.8 %copy.6 = f32[32,32,128]{2,1,0:T(8,128)} copy(f32[32,32,128]{2,1,0:T(8,128)S(1)} %bitcast.3) | data formatting | bytes 1048576
